TPU v7x, 512 devices: a whole 4x4x16 slice. The times are simulated.
512 devices in a mesh: ctx: 64 (over z, y), head: 8 (over x, core).
Axes of the slice: x: 4, y: 4, z: 16, core: 2. Of those that a mesh axis runs over, the one named last changes fastest.
Arguments:
- queries: bfloat16 [65536, 2048], P(('ctx', 'head')), may hold values from -240 to 240
- key_rows: bfloat16 [65536, 1024], P(('ctx', 'head')), may hold values from -6 to 6
- value_rows: bfloat16 [65536, 1024], P(('ctx', 'head')), may hold values from -6 to 6
- grad_out: bfloat16 [65536, 2048], P(('ctx', 'head')), may hold values from -6 to 6
- doc_start: int32 [65536], P('ctx'), may hold values from 0 to 65535, as said below
- reach_end: int32 [65536], P('ctx'), may hold values from 0 to 65535, as said below
Outputs:
- attended: bfloat16 [65536, 2048], P(('ctx', 'head'))
- grad_queries: bfloat16 [65536, 2048], P(('ctx', 'head'))
- grad_keys: bfloat16 [65536, 1024], P(('ctx', 'head'))
- grad_values: bfloat16 [65536, 1024], P(('ctx', 'head'))
Inputs may be any that keep to these rules, and one draw needn't show every extreme that they name: Non-decreasing; doc_start[t] <= t and doc_start[t] is the position of a token whose doc_start is itself. Documents hold at most 1024 tokens, some document exactly that many; all but the last hold 256 or more. t <= reach_end[t] < t + 256, and reach_end[t] lies in t's document. Image tokens form spans of up to 256 tokens inside one document, some span exactly 256; every token of a span has the span's last position as reach_end. Each span starts fewer than 256 tokens before the end of a context shard's 1024 tokens and ends at or after that end.
All inputs are finite; a program needn't handle non-finite values.
Results may differ from a plain program's by a relative error of at most 0.03.
Values may be sent and summed in bfloat16 or wider, within the bound.
A program may use at most 128 MiB of HBM per device.

v0:
```python
import jax
import jax.numpy as jnp
from jax import lax
from jax.sharding import PartitionSpec as P

HD = 128
SPAN = 256


query_scale = 168.0 ** (-0.5)


def shifted(value, axis, by):
    length = lax.axis_size(axis)
    pairs = [(i, i + by) for i in range(length) if 0 <= i + by < length]
    return lax.ppermute(value, axis, pairs)


def product(left, right, dims):
    return lax.dot_general(left, right, (dims, ((), ())), preferred_element_type=jnp.float32)


def local(queries, key_rows, value_rows, grad_out, doc_start, reach_end):
    q_local, k_local, v_local, g_local = (
        lax.all_to_all(queries, "head", split_axis=1, concat_axis=0, tiled=True),
        lax.all_to_all(key_rows, "head", split_axis=1, concat_axis=0, tiled=True),
        lax.all_to_all(value_rows, "head", split_axis=1, concat_axis=0, tiled=True),
        lax.all_to_all(grad_out, "head", split_axis=1, concat_axis=0, tiled=True),
    )
    prior = shifted((k_local, v_local), "ctx", 1)
    rows = q_local.shape[0]
    span_rows = SPAN
    start_pos = lax.axis_index("ctx") * rows
    ahead = shifted((k_local[:span_rows], v_local[:span_rows]), "ctx", -1)
    key_parts = [prior[0], k_local, ahead[0]]
    value_parts = [prior[1], v_local, ahead[1]]
    lengths = [rows, rows, span_rows]
    offsets = [0, rows, 2 * rows]
    window = 2 * rows + span_rows
    key_place = start_pos - rows + jnp.arange(window, dtype=jnp.int32)
    block_rows = 512
    local_heads = q_local.shape[1] // HD
    local_groups = k_local.shape[1] // HD
    group = local_heads // local_groups
    key_terms = [[jnp.zeros((lengths[part], HD), jnp.float32) for part in range(3)]]
    value_terms = [[jnp.zeros((lengths[part], HD), jnp.float32) for part in range(3)]]
    attended_blocks = []
    grad_query_blocks = []
    for block_first in range(0, rows, block_rows):
        lower = doc_start[block_first : block_first + block_rows]
        upper = reach_end[block_first : block_first + block_rows]
        allowed = (key_place[None, :] >= lower[:, None]) & (key_place[None, :] <= upper[:, None])
        attended_heads = []
        grad_query_heads = []
        for head_index in range(local_heads):
            kv_index = head_index // group
            query_head = q_local[
                block_first : block_first + block_rows, head_index * HD : (head_index + 1) * HD
            ]
            grad_head = g_local[
                block_first : block_first + block_rows, head_index * HD : (head_index + 1) * HD
            ]
            key_heads = [piece for piece in key_parts]
            value_heads = [piece for piece in value_parts]
            scores = (
                jnp.concatenate(
                    [product(query_head, key_heads[part], ((1,), (1,))) for part in range(3)],
                    axis=1,
                )
                * query_scale
            )
            scores = jnp.where(allowed, scores, -jnp.inf)
            top = jnp.max(scores, axis=-1, keepdims=True)
            total = jnp.sum(jnp.exp(scores - top), axis=-1, keepdims=True)
            probs = jnp.exp(scores - (top + jnp.log(total)))
            probs_low = probs.astype(jnp.bfloat16)
            attended_sum = product(
                probs_low[:, offsets[0] : offsets[0] + lengths[0]], value_heads[0], ((1,), (0,))
            )
            for part in range(1, 3):
                attended_sum = attended_sum + product(
                    probs_low[:, offsets[part] : offsets[part] + lengths[part]],
                    value_heads[part],
                    ((1,), (0,)),
                )
            attended_head = attended_sum.astype(jnp.bfloat16)
            grad_probs = jnp.concatenate(
                [product(grad_head, value_heads[part], ((1,), (1,))) for part in range(3)], axis=1
            )
            delta = jnp.sum(
                grad_head.astype(jnp.float32) * attended_head.astype(jnp.float32),
                axis=-1,
                keepdims=True,
            )
            grad_scores = (query_scale * probs * (grad_probs - delta)).astype(jnp.bfloat16)
            grad_query_sum = product(
                grad_scores[:, offsets[0] : offsets[0] + lengths[0]], key_heads[0], ((1,), (0,))
            )
            for part in range(1, 3):
                grad_query_sum = grad_query_sum + product(
                    grad_scores[:, offsets[part] : offsets[part] + lengths[part]],
                    key_heads[part],
                    ((1,), (0,)),
                )
            for part in range(3):
                score_cols = grad_scores[:, offsets[part] : offsets[part] + lengths[part]]
                prob_cols = probs_low[:, offsets[part] : offsets[part] + lengths[part]]
                key_terms[kv_index][part] = key_terms[kv_index][part] + product(
                    score_cols, query_head, ((0,), (0,))
                )
                value_terms[kv_index][part] = value_terms[kv_index][part] + product(
                    prob_cols, grad_head, ((0,), (0,))
                )
            attended_heads.append(attended_head)
            grad_query_heads.append(grad_query_sum.astype(jnp.bfloat16))
        attended_blocks.append(jnp.concatenate(attended_heads, axis=1))
        grad_query_blocks.append(jnp.concatenate(grad_query_heads, axis=1))
    key_pieces = [key_terms[0][part] for part in range(3)]
    value_pieces = [value_terms[0][part] for part in range(3)]
    returned = shifted((key_pieces[0], value_pieces[0]), "ctx", -1)
    behind = (
        shifted(key_pieces[2].astype(jnp.bfloat16), "ctx", 1).astype(jnp.float32),
        shifted(value_pieces[2].astype(jnp.bfloat16), "ctx", 1).astype(jnp.float32),
    )
    grad_key_sum = key_pieces[1] + returned[0] + jnp.pad(behind[0], ((0, rows - span_rows), (0, 0)))
    grad_value_sum = (
        value_pieces[1] + returned[1] + jnp.pad(behind[1], ((0, rows - span_rows), (0, 0)))
    )
    attended_all = jnp.concatenate(attended_blocks, axis=0)
    grad_query_all = jnp.concatenate(grad_query_blocks, axis=0)
    attended, grad_queries, grad_keys, grad_values = (
        lax.all_to_all(attended_all, "head", split_axis=0, concat_axis=1, tiled=True),
        lax.all_to_all(grad_query_all, "head", split_axis=0, concat_axis=1, tiled=True),
        lax.all_to_all(
            grad_key_sum.astype(jnp.bfloat16), "head", split_axis=0, concat_axis=1, tiled=True
        ),
        lax.all_to_all(
            grad_value_sum.astype(jnp.bfloat16), "head", split_axis=0, concat_axis=1, tiled=True
        ),
    )
    return (attended, grad_queries, grad_keys, grad_values)


def solution(mesh):
    return jax.shard_map(
        local,
        mesh=mesh,
        in_specs=(
            P(("ctx", "head"), None),
            P(("ctx", "head"), None),
            P(("ctx", "head"), None),
            P(("ctx", "head"), None),
            P("ctx"),
            P("ctx"),
        ),
        out_specs=(
            P(("ctx", "head"), None),
            P(("ctx", "head"), None),
            P(("ctx", "head"), None),
            P(("ctx", "head"), None),
        ),
        check_vma=False,
    )
```

profile of v0, /device:TPU:128, one launch (start us, length us, event | category | flops | bytes accessed | tf_op | source)
XLA Modules:
  0.0 235.7 jit_solution(18418985022277114899)
XLA Ops:
  0.7 1.9 copy.59
  2.5 4.4 %all-to-all-start.1 = ((bf16[128,8,128]{0,2,1:T(8,128)(2,1)}), bf16[128,8,128]{0,2,1:T(8,128)(2,1)S(1)}, u32[]{:S(2)}, u32[]{:S(2)}) async-start(bf16[128,8,128]{0,2,1:T(8,128)(2,1)} %bitcast.3), calls=%async_computation.1 | async-start | bytes 524288 | tf_op jit(solution)/shard_map/all_to_all | solution.py:26
  7.0 1.8 copy.63
  8.8 5.7 %all-to-all-done.1 = bf16[128,8,128]{0,2,1:T(8,128)(2,1)S(1)} async-done(((bf16[128,8,128]{0,2,1:T(8,128)(2,1)}), bf16[128,8,128]{0,2,1:T(8,128)(2,1)S(1)}, u32[]{:S(2)}, u32[]{:S(2)}) %all-to-all-start.1) | async-done | bytes 262176 | tf_op jit(solution)/shard_map/all_to_all | solution.py:26
  14.5 3.4 %all-to-all-start.2 = ((bf16[128,8,128]{0,2,1:T(8,128)(2,1)}), bf16[128,8,128]{0,2,1:T(8,128)(2,1)S(1)}, u32[]{:S(2)}, u32[]{:S(2)}) async-start(bf16[128,8,128]{0,2,1:T(8,128)(2,1)} %bitcast.7), calls=%async_computation.2 | async-start | bytes 524288 | tf_op jit(solution)/shard_map/all_to_all | solution.py:27
  18.9 6.4 %all-to-all-done.2 = bf16[128,8,128]{0,2,1:T(8,128)(2,1)S(1)} async-done(((bf16[128,8,128]{0,2,1:T(8,128)(2,1)}), bf16[128,8,128]{0,2,1:T(8,128)(2,1)S(1)}, u32[]{:S(2)}, u32[]{:S(2)}) %all-to-all-start.2) | async-done | bytes 262176 | tf_op jit(solution)/shard_map/all_to_all | solution.py:27
  25.4 3.5 %all-to-all-start = ((bf16[128,8,256]{0,2,1:T(8,128)(2,1)}), bf16[128,8,256]{0,2,1:T(8,128)(2,1)S(1)}, u32[]{:S(2)}, u32[]{:S(2)}) async-start(bf16[128,8,256]{0,2,1:T(8,128)(2,1)} %bitcast), calls=%async_computation | async-start | bytes 1048576 | tf_op jit(solution)/shard_map/all_to_all | solution.py:25
  31.5 3.5 %collective-permute-start = (bf16[1024,128]{1,0:T(8,128)(2,1)S(1)}, bf16[1024,128]{1,0:T(8,128)(2,1)S(1)}, u32[]{:S(2)}, u32[]{:S(2)}) collective-permute-start(bf16[1024,128]{1,0:T(8,128)(2,1)S(1)} %bitcast.96), channel_id=1, source_target_pairs={{0,8},{8,16},{16,24},{24,32},{32,40},{40,48},{48,56},{56,64},{64,7... | collective-permute-start | bytes 786440 | tf_op jit(solution)/shard_map/ppermute | solution.py:16
  35.8 5.7 %collective-permute-start.1 = (bf16[256,128]{1,0:T(8,128)(2,1)}, bf16[256,128]{1,0:T(8,128)(2,1)S(1)}, u32[]{:S(2)}, u32[]{:S(2)}) collective-permute-start(bf16[256,128]{1,0:T(8,128)(2,1)} %bitcast.6), channel_id=1, source_target_pairs={{8,0},{16,8},{24,16},{32,24},{40,32},{48,40},{56,48},{64,56},{72,6... | collective-permute-start | bytes 196616 | tf_op jit(solution)/shard_map/ppermute | solution.py:16
  42.2 1.9 collective-permute-start.3
  44.1 3.9 %collective-permute-start.2 = (bf16[1024,128]{1,0:T(8,128)(2,1)S(1)}, bf16[1024,128]{1,0:T(8,128)(2,1)}, u32[]{:S(2)}, u32[]{:S(2)}) collective-permute-start(bf16[1024,128]{1,0:T(8,128)(2,1)S(1)} %bitcast.105), channel_id=1, source_target_pairs={{0,8},{8,16},{16,24},{24,32},{32,40},{40,48},{48,56},{56,64},{64,7... | collective-permute-start | bytes 786440 | tf_op jit(solution)/shard_map/ppermute | solution.py:16
  48.0 4.7 %all-to-all-start.4 = ((bf16[128,8,256]{0,2,1:T(8,128)(2,1)}), bf16[128,8,256]{0,2,1:T(8,128)(2,1)}, u32[]{:S(2)}, u32[]{:S(2)}) async-start(bf16[128,8,256]{0,2,1:T(8,128)(2,1)} %bitcast.13), calls=%async_computation.4 | async-start | bytes 1048576 | tf_op jit(solution)/shard_map/all_to_all | solution.py:28
  53.4 1.8 fusion.124
  55.2 1.7 fusion.133
  56.9 1.8 fusion.142
  58.7 4.5 %all-to-all-done.4 = bf16[128,8,256]{0,2,1:T(8,128)(2,1)} async-done(((bf16[128,8,256]{0,2,1:T(8,128)(2,1)}), bf16[128,8,256]{0,2,1:T(8,128)(2,1)}, u32[]{:S(2)}, u32[]{:S(2)}) %all-to-all-start.4) | async-done | bytes 524320 | tf_op jit(solution)/shard_map/all_to_all | solution.py:28
  64.3 1.8 fusion.169
  66.1 1.8 fusion.178
  67.9 1.8 fusion.151
  69.7 1.8 fusion.160
  78.3 1.8 fusion.117
  80.0 1.8 fusion.126
  81.8 1.8 fusion.135
  83.6 1.8 fusion.144
  85.5 7.4 %fusion.182 = (f32[512]{0:T(512)S(1)}, f32[512,2304]{1,0:T(8,128)S(1)}, f32[512]{0:T(512)S(1)}, f32[512,2304]{1,0:T(8,128)S(1)}, f32[512]{0:T(512)S(1)}, /*index...) fusion(f32[512,256]{1,0:T(8,128)} %fusion.140, f32[512,1024]{1,0:T(8,128)} %fusion.142, ...), kind=kLoop, calls=%fused_computation.242 | loop fusion | flops 30668800 | bytes 37774336 | tf_op jit(solution)/shard_map/reduce_max | solution.py:73
  95.5 1.3 fusion.77
  96.8 1.3 fusion.81
  106.0 2.8 %fusion.171 = f32[512,1024]{1,0:T(8,128)} fusion(bf16[1024,128]{1,0:T(8,128)(2,1)} %collective-permute-done.2, bf16[1024,256]{0,1:T(8,128)(2,1)S(1)} %copy_bitcast_fusion), kind=kOutput, calls=%fused_computation.226 | convolution fusion | flops 134217728 | bytes 2490368 | tf_op jit(solution)/shard_map/dot_general | solution.py:20
  108.8 2.7 %fusion.180 = f32[512,1024]{1,0:T(8,128)} fusion(bf16[1024,128]{1,0:T(8,128)(2,1)} %collective-permute-done.2, bf16[1024,256]{0,1:T(8,128)(2,1)S(1)} %copy_bitcast_fusion), kind=kOutput, calls=%fused_computation.235 | convolution fusion | flops 134217728 | bytes 2490368 | tf_op jit(solution)/shard_map/dot_general | solution.py:20
  111.5 1.4 fusion.31
  113.0 1.5 fusion.32
  114.5 1.5 fusion.33
  116.0 2.3 multiply_reduce_fusion.3
  118.3 7.7 %fusion.5 = (bf16[512,2304]{1,0:T(8,128)(2,1)}, bf16[512,2304]{1,0:T(8,128)(2,1)}) fusion(f32[512,256]{1,0:T(8,128)} %fusion.176, f32[512,1024]{1,0:T(8,128)} %fusion.178, f32[512,1024]{1,0:T(8,128)} %fusion.180, f32[512,2304]{1,0:T(8,128)S(1)} %get-tuple-element.13, f32[512]{0:T(512)S(1)} %get-tuple-element.8, f32[512]{0:T(512)S(1)} %log_add_fusion.3, ...), kind=kLoop, calls=%fused_computation.10 | loop fusion | flops 16515072 | bytes 23601152 | tf_op jit(solution)/shard_map/convert_element_type | solution.py:95
  127.2 2.6 %fusion.55 = f32[1024,128]{1,0:T(8,128)} fusion(bf16[512,2304]{1,0:T(8,128)(2,1)} %get-tuple-element.33, bf16[1024,256]{1,0:T(8,128)(2,1)S(1)} %bitcast.127), kind=kOutput, calls=%fused_computation.99 | convolution fusion | flops 134217728 | bytes 1703936 | tf_op jit(solution)/shard_map/dot_general | solution.py:20
  129.9 2.6 %fusion.59 = f32[1024,128]{1,0:T(8,128)} fusion(bf16[512,2304]{1,0:T(8,128)(2,1)} %get-tuple-element.33, bf16[1024,256]{1,0:T(8,128)(2,1)S(1)} %bitcast.128), kind=kOutput, calls=%fused_computation.103 | convolution fusion | flops 134217728 | bytes 1703936 | tf_op jit(solution)/shard_map/dot_general | solution.py:20
  132.5 2.4 %fusion.57 = f32[512,128]{0,1:T(8,128)} fusion(bf16[1024,128]{1,0:T(8,128)(2,1)S(1)} %bitcast.101, bf16[512,2304]{1,0:T(8,128)(2,1)} %get-tuple-element.33), kind=kOutput, calls=%fused_computation.101 | convolution fusion | flops 134217728 | bytes 1572864 | tf_op jit(solution)/shard_map/dot_general | solution.py:20
  136.4 1.9 collective-permute-start.7
  138.3 1.3 convolution_add_fusion.5
  140.6 1.3 convolution_add_fusion
  141.9 7.2 %collective-permute-start.6 = (f32[1024,128]{1,0:T(8,128)}, f32[1024,128]{1,0:T(8,128)}, u32[]{:S(2)}, u32[]{:S(2)}) collective-permute-start(f32[1024,128]{1,0:T(8,128)} %convolution_add_fusion), channel_id=1, source_target_pairs={{8,0},{16,8},{24,16},{32,24},{40,32},{48,40},{56,48},{64,56},{72,6... | collective-permute-start | bytes 1572872 | tf_op jit(solution)/shard_map/ppermute | solution.py:16
  150.6 2.8 %fusion.153 = f32[512,1024]{1,0:T(8,128)} fusion(bf16[1024,128]{1,0:T(8,128)(2,1)} %collective-permute-done.2, bf16[1024,256]{0,1:T(8,128)(2,1)S(1)} %copy-done.9), kind=kOutput, calls=%fused_computation.208 | convolution fusion | flops 134217728 | bytes 2490368 | tf_op jit(solution)/shard_map/dot_general | solution.py:20
  153.4 2.7 %fusion.162 = f32[512,1024]{1,0:T(8,128)} fusion(bf16[1024,128]{1,0:T(8,128)(2,1)} %collective-permute-done.2, bf16[1024,256]{0,1:T(8,128)(2,1)S(1)} %copy-done.9), kind=kOutput, calls=%fused_computation.217 | convolution fusion | flops 134217728 | bytes 2490368 | tf_op jit(solution)/shard_map/dot_general | solution.py:20
  156.1 5.8 %fusion.9 = (bf16[512,2304]{1,0:T(8,128)(2,1)}, bf16[512,2304]{1,0:T(8,128)(2,1)S(1)}) fusion(f32[512,256]{1,0:T(8,128)} %fusion.158, f32[512,1024]{1,0:T(8,128)} %fusion.160, f32[512,1024]{1,0:T(8,128)} %fusion.162, f32[512,2304]{1,0:T(8,128)S(1)} %get-tuple-element.27, f32[512]{0:T(512)S(1)} %get-tuple-element.10, f32[512]{0:T(512)S(1)} %log_add_fusion.1, ...), kind=kLoop, calls=%fused_computation.16 | loop fusion | flops 16515072 | bytes 23601152 | tf_op jit(solution)/shard_map/convert_element_type | solution.py:95
  162.0 2.6 %fusion.46 = f32[512,128]{0,1:T(8,128)S(1)} fusion(bf16[1024,128]{1,0:T(8,128)(2,1)S(1)} %bitcast.103, bf16[512,2304]{1,0:T(8,128)(2,1)} %get-tuple-element.35), kind=kOutput, calls=%fused_computation.90 | convolution fusion | flops 134217728 | bytes 1572864 | tf_op jit(solution)/shard_map/dot_general | solution.py:20
  167.2 2.0 collective-permute-start.5
  169.7 1.3 convolution_add_fusion.7
  174.9 4.3 %all-to-all-start.5 = ((bf16[8,128,256]{1,2,0:T(8,128)(2,1)}), bf16[8,128,256]{1,2,0:T(8,128)(2,1)}, u32[]{:S(2)}, u32[]{:S(2)}) async-start(bf16[8,128,256]{1,2,0:T(8,128)(2,1)} %copy_bitcast_fusion.1), calls=%async_computation.5 | async-start | bytes 1048576 | tf_op jit(solution)/shard_map/all_to_all | solution.py:133
  179.2 2.7 %convolution_add_fusion.6 = f32[1024,128]{1,0:T(8,128)} fusion(f32[1024,128]{1,0:T(8,128)} %convolution_add_fusion.7, bf16[512,2304]{1,0:T(8,128)(2,1)} %copy-done.4, bf16[1024,256]{1,0:T(8,128)(2,1)S(1)} %bitcast.134), kind=kOutput, calls=%fused_computation.40 | convolution fusion | flops 134348800 | bytes 2228224 | tf_op jit(solution)/shard_map/dot_general | solution.py:20
  181.9 7.2 %collective-permute-start.4 = (f32[1024,128]{1,0:T(8,128)}, f32[1024,128]{1,0:T(8,128)}, u32[]{:S(2)}, u32[]{:S(2)}) collective-permute-start(f32[1024,128]{1,0:T(8,128)} %convolution_add_fusion.6), channel_id=1, source_target_pairs={{8,0},{16,8},{24,16},{32,24},{40,32},{48,40},{56,48},{64,56},{72,6... | collective-permute-start | bytes 1572872 | tf_op jit(solution)/shard_map/ppermute | solution.py:16
  189.1 1.9 copy_bitcast_fusion.2
  191.1 2.5 %convolution_add_fusion.4 = f32[1024,128]{1,0:T(8,128)} fusion(f32[1024,128]{1,0:T(8,128)S(1)} %copy-done.14, bf16[512,2304]{1,0:T(8,128)(2,1)} %copy-done.1, bf16[1024,256]{0,1:T(8,128)(2,1)S(1)} %copy-done.10), kind=kOutput, calls=%fused_computation.38 | convolution fusion | flops 134348800 | bytes 2228224 | tf_op jit(solution)/shard_map/dot_general | solution.py:20
  193.6 4.7 %all-to-all-start.3 = ((bf16[8,128,256]{1,2,0:T(8,128)(2,1)}), bf16[8,128,256]{1,2,0:T(8,128)(2,1)}, u32[]{:S(2)}, u32[]{:S(2)}) async-start(bf16[8,128,256]{1,2,0:T(8,128)(2,1)} %copy_bitcast_fusion.2), calls=%async_computation.3 | async-start | bytes 1048576 | tf_op jit(solution)/shard_map/all_to_all | solution.py:132
  198.3 1.8 convolution_add_fusion.11
  200.1 2.5 %convolution_add_fusion.10 = f32[1024,128]{1,0:T(8,128)} fusion(f32[1024,128]{1,0:T(8,128)S(1)} %convolution_add_fusion.11, bf16[512,2304]{1,0:T(8,128)(2,1)} %get-tuple-element.35, bf16[1024,256]{1,0:T(8,128)(2,1)S(1)} %bitcast.136), kind=kOutput, calls=%fused_computation.44 | convolution fusion | flops 134348800 | bytes 2228224 | tf_op jit(solution)/shard_map/dot_general | solution.py:20
  202.6 2.0 copy.80
  204.7 4.1 %all-to-all-done.3 = bf16[8,128,256]{1,2,0:T(8,128)(2,1)} async-done(((bf16[8,128,256]{1,2,0:T(8,128)(2,1)}), bf16[8,128,256]{1,2,0:T(8,128)(2,1)}, u32[]{:S(2)}, u32[]{:S(2)}) %all-to-all-start.3) | async-done | bytes 524320 | tf_op jit(solution)/shard_map/all_to_all | solution.py:132
  208.7 2.0 copy.79
  210.8 2.4 %fusion.20 = bf16[1024,128]{1,0:T(8,128)(2,1)} fusion(f32[1024,128]{1,0:T(8,128)} %collective-permute-done.6, f32[1024,128]{1,0:T(8,128)} %convolution_add_fusion.4, bf16[512,2304]{1,0:T(8,128)(2,1)S(1)} %fusion.15, bf16[256,128]{1,0:T(8,128)(2,1)} %collective-permute-done.7, bf16[1024,256]{0,1:T(8,128)(2,1)S(1)} %copy-done.10), kind=kOutput, calls=%fused_computation.50 | convolution fusion | flops 134873088 | bytes 2555904 | tf_op jit(solution)/shard_map/dot_general | solution.py:20
  213.2 3.4 %all-to-all-start.7 = ((bf16[8,128,128]{2,1,0:T(8,128)(2,1)}), bf16[8,128,128]{2,1,0:T(8,128)(2,1)S(1)}, u32[]{:S(2)}, u32[]{:S(2)}) async-start(bf16[8,128,128]{2,1,0:T(8,128)(2,1)} %bitcast.143), calls=%async_computation.7 | async-start | bytes 524288 | tf_op jit(solution)/shard_map/all_to_all | solution.py:137
  216.6 2.7 %fusion.21 = bf16[1024,128]{1,0:T(8,128)(2,1)} fusion(f32[1024,128]{1,0:T(8,128)} %collective-permute-done.4, f32[1024,128]{1,0:T(8,128)} %convolution_add_fusion.10, bf16[512,2304]{1,0:T(8,128)(2,1)} %copy-done.4, bf16[256,128]{1,0:T(8,128)(2,1)} %collective-permute-done.5, bf16[1024,256]{1,0:T(8,128)(2,1)S(1)} %bitcast.137), kind=kOutput, calls=%fused_computation.51 | convolution fusion | flops 134873088 | bytes 2555904 | tf_op jit(solution)/shard_map/dot_general | solution.py:20
  219.3 4.7 %all-to-all-done.7 = bf16[8,128,128]{2,1,0:T(8,128)(2,1)S(1)} async-done(((bf16[8,128,128]{2,1,0:T(8,128)(2,1)}), bf16[8,128,128]{2,1,0:T(8,128)(2,1)S(1)}, u32[]{:S(2)}, u32[]{:S(2)}) %all-to-all-start.7) | async-done | bytes 262176 | tf_op jit(solution)/shard_map/all_to_all | solution.py:137
  224.0 3.4 %all-to-all-start.6 = ((bf16[8,128,128]{2,1,0:T(8,128)(2,1)}), bf16[8,128,128]{2,1,0:T(8,128)(2,1)S(1)}, u32[]{:S(2)}, u32[]{:S(2)}) async-start(bf16[8,128,128]{2,1,0:T(8,128)(2,1)} %bitcast.17), calls=%async_computation.6 | async-start | bytes 524288 | tf_op jit(solution)/shard_map/all_to_all | solution.py:134
  228.2 6.7 %all-to-all-done.6 = bf16[8,128,128]{2,1,0:T(8,128)(2,1)S(1)} async-done(((bf16[8,128,128]{2,1,0:T(8,128)(2,1)}), bf16[8,128,128]{2,1,0:T(8,128)(2,1)S(1)}, u32[]{:S(2)}, u32[]{:S(2)}) %all-to-all-start.6) | async-done | bytes 262176 | tf_op jit(solution)/shard_map/all_to_all | solution.py:134
  (140 shorter events, 37.4 us)
Async XLA Ops:
  0.6 17.3 %copy-start.20 = (bf16[128,2048]{1,0:T(8,128)(2,1)S(1)}, bf16[128,2048]{1,0:T(8,128)(2,1)}, u32[]{:S(2)}) copy-start(bf16[128,2048]{1,0:T(8,128)(2,1)} %param.6) | copy-start | bytes 1572868
  0.6 28.3 %copy-start.21 = (bf16[128,2048]{1,0:T(8,128)(2,1)S(1)}, bf16[128,2048]{1,0:T(8,128)(2,1)}, u32[]{:S(2)}) copy-start(bf16[128,2048]{1,0:T(8,128)(2,1)} %param.9) | copy-start | bytes 1572868
  2.5 27.4 %copy-start.30 = (s32[1024]{0:T(1024)S(1)}, s32[1024]{0:T(1024)}, u32[]{:S(2)}) copy-start(s32[1024]{0:T(1024)} %param.10) | copy-start | bytes 12292
  2.5 28.0 %copy-start.31 = (s32[1024]{0:T(1024)S(1)}, s32[1024]{0:T(1024)}, u32[]{:S(2)}) copy-start(s32[1024]{0:T(1024)} %param.11) | copy-start | bytes 12292
  2.5 12.0 %all-to-all-start.1 = ((bf16[128,8,128]{0,2,1:T(8,128)(2,1)}), bf16[128,8,128]{0,2,1:T(8,128)(2,1)S(1)}, u32[]{:S(2)}, u32[]{:S(2)}) async-start(bf16[128,8,128]{0,2,1:T(8,128)(2,1)} %bitcast.3), calls=%async_computation.1 | async-start | bytes 524288 | tf_op jit(solution)/shard_map/all_to_all | solution.py:26
  14.5 10.9 %all-to-all-start.2 = ((bf16[128,8,128]{0,2,1:T(8,128)(2,1)}), bf16[128,8,128]{0,2,1:T(8,128)(2,1)S(1)}, u32[]{:S(2)}, u32[]{:S(2)}) async-start(bf16[128,8,128]{0,2,1:T(8,128)(2,1)} %bitcast.7), calls=%async_computation.2 | async-start | bytes 524288 | tf_op jit(solution)/shard_map/all_to_all | solution.py:27
  25.4 22.6 %all-to-all-start = ((bf16[128,8,256]{0,2,1:T(8,128)(2,1)}), bf16[128,8,256]{0,2,1:T(8,128)(2,1)S(1)}, u32[]{:S(2)}, u32[]{:S(2)}) async-start(bf16[128,8,256]{0,2,1:T(8,128)(2,1)} %bitcast), calls=%async_computation | async-start | bytes 1048576 | tf_op jit(solution)/shard_map/all_to_all | solution.py:25
  31.5 46.8 %collective-permute-start = (bf16[1024,128]{1,0:T(8,128)(2,1)S(1)}, bf16[1024,128]{1,0:T(8,128)(2,1)S(1)}, u32[]{:S(2)}, u32[]{:S(2)}) collective-permute-start(bf16[1024,128]{1,0:T(8,128)(2,1)S(1)} %bitcast.96), channel_id=1, source_target_pairs={{0,8},{8,16},{16,24},{24,32},{32,40},{40,48},{48,56},{56,64},{64,7... | collective-permute-start | bytes 786440 | tf_op jit(solution)/shard_map/ppermute | solution.py:16
  35.8 35.7 %collective-permute-start.1 = (bf16[256,128]{1,0:T(8,128)(2,1)}, bf16[256,128]{1,0:T(8,128)(2,1)S(1)}, u32[]{:S(2)}, u32[]{:S(2)}) collective-permute-start(bf16[256,128]{1,0:T(8,128)(2,1)} %bitcast.6), channel_id=1, source_target_pairs={{8,0},{16,8},{24,16},{32,24},{40,32},{48,40},{56,48},{64,56},{72,6... | collective-permute-start | bytes 196616 | tf_op jit(solution)/shard_map/ppermute | solution.py:16
  42.2 31.8 %collective-permute-start.3 = (bf16[256,128]{1,0:T(8,128)(2,1)}, bf16[256,128]{1,0:T(8,128)(2,1)S(1)}, u32[]{:S(2)}, u32[]{:S(2)}) collective-permute-start(bf16[256,128]{1,0:T(8,128)(2,1)} %bitcast.10), channel_id=1, source_target_pairs={{8,0},{16,8},{24,16},{32,24},{40,32},{48,40},{56,48},{64,56},{72,6... | collective-permute-start | bytes 196616 | tf_op jit(solution)/shard_map/ppermute | solution.py:16
  44.1 61.9 %collective-permute-start.2 = (bf16[1024,128]{1,0:T(8,128)(2,1)S(1)}, bf16[1024,128]{1,0:T(8,128)(2,1)}, u32[]{:S(2)}, u32[]{:S(2)}) collective-permute-start(bf16[1024,128]{1,0:T(8,128)(2,1)S(1)} %bitcast.105), channel_id=1, source_target_pairs={{0,8},{8,16},{16,24},{24,32},{32,40},{40,48},{48,56},{56,64},{64,7... | collective-permute-start | bytes 786440 | tf_op jit(solution)/shard_map/ppermute | solution.py:16
  48.0 15.1 %all-to-all-start.4 = ((bf16[128,8,256]{0,2,1:T(8,128)(2,1)}), bf16[128,8,256]{0,2,1:T(8,128)(2,1)}, u32[]{:S(2)}, u32[]{:S(2)}) async-start(bf16[128,8,256]{0,2,1:T(8,128)(2,1)} %bitcast.13), calls=%async_computation.4 | async-start | bytes 1048576 | tf_op jit(solution)/shard_map/all_to_all | solution.py:28
  64.3 51.7 %copy-start.8 = (bf16[1024,256]{0,1:T(8,128)(2,1)}, bf16[1024,256]{0,1:T(8,128)(2,1)S(1)}, u32[]{:S(2)}) copy-start(bf16[1024,256]{0,1:T(8,128)(2,1)S(1)} %copy_bitcast_fusion) | copy-start | bytes 1572868
  78.3 5.4 %copy-start.11 = (bf16[1024,128]{1,0:T(8,128)(2,1)}, bf16[1024,128]{1,0:T(8,128)(2,1)S(1)}, u32[]{:S(2)}) copy-start(bf16[1024,128]{1,0:T(8,128)(2,1)S(1)} %collective-permute-done) | copy-start | bytes 786436
  81.8 3.7 %copy-start.27 = (s32[512]{0:T(512)S(1)}, s32[512]{0:T(512)}, u32[]{:S(2)}) copy-start(s32[512]{0:T(512)} %get-tuple-element.29) | copy-start | bytes 6148
  81.8 3.7 %copy-start.28 = (s32[512]{0:T(512)S(1)}, s32[512]{0:T(512)}, u32[]{:S(2)}) copy-start(s32[512]{0:T(512)} %get-tuple-element.30) | copy-start | bytes 6148
  81.8 3.7 %copy-start.29 = (s32[512]{0:T(512)S(1)}, s32[512]{0:T(512)}, u32[]{:S(2)}) copy-start(s32[512]{0:T(512)} %get-tuple-element.31) | copy-start | bytes 6148
  92.9 6.5 %copy-start = (f32[512,2304]{1,0:T(8,128)}, f32[512,2304]{1,0:T(8,128)S(1)}, u32[]{:S(2)}) copy-start(f32[512,2304]{1,0:T(8,128)S(1)} %get-tuple-element.21) | copy-start | bytes 14155780
  100.2 11.3 %copy-start.6 = (bf16[512,2304]{1,0:T(8,128)(2,1)}, bf16[512,2304]{1,0:T(8,128)(2,1)S(1)}, u32[]{:S(2)}) copy-start(bf16[512,2304]{1,0:T(8,128)(2,1)S(1)} %fusion.13) | copy-start | bytes 7077892
  101.9 11.1 %copy-start.1 = (bf16[512,2304]{1,0:T(8,128)(2,1)}, bf16[512,2304]{1,0:T(8,128)(2,1)S(1)}, u32[]{:S(2)}) copy-start(bf16[512,2304]{1,0:T(8,128)(2,1)S(1)} %fusion.14) | copy-start | bytes 7077892
  113.0 5.3 %copy-start.22 = (bf16[512,128]{0,1:T(8,128)(2,1)}, bf16[512,128]{0,1:T(8,128)(2,1)S(1)}, u32[]{:S(2)}) copy-start(bf16[512,128]{0,1:T(8,128)(2,1)S(1)} %fusion.31) | copy-start | bytes 393220
  114.5 11.5 %copy-start.24 = (bf16[512,128]{0,1:T(8,128)(2,1)}, bf16[512,128]{0,1:T(8,128)(2,1)S(1)}, u32[]{:S(2)}) copy-start(bf16[512,128]{0,1:T(8,128)(2,1)S(1)} %fusion.32) | copy-start | bytes 393220
  116.0 2.3 copy-start.25
  127.2 7.7 %copy-start.7 = (bf16[512,2304]{1,0:T(8,128)(2,1)S(1)}, bf16[512,2304]{1,0:T(8,128)(2,1)}, u32[]{:S(2)}) copy-start(bf16[512,2304]{1,0:T(8,128)(2,1)} %copy-done.6) | copy-start | bytes 7077892
  127.2 7.7 %copy-start.9 = (bf16[1024,256]{0,1:T(8,128)(2,1)S(1)}, bf16[1024,256]{0,1:T(8,128)(2,1)}, u32[]{:S(2)}) copy-start(bf16[1024,256]{0,1:T(8,128)(2,1)} %copy-done.8) | copy-start | bytes 1572868
  127.2 7.7 %copy-start.26 = (f32[256,128]{1,0:T(8,128)S(1)}, f32[256,128]{1,0:T(8,128)}, u32[]{:S(2)}) copy-start(f32[256,128]{1,0:T(8,128)} %fusion.106) | copy-start | bytes 393220
  129.9 5.3 %copy-start.2 = (bf16[512,2304]{1,0:T(8,128)(2,1)S(1)}, bf16[512,2304]{1,0:T(8,128)(2,1)}, u32[]{:S(2)}) copy-start(bf16[512,2304]{1,0:T(8,128)(2,1)} %copy-done.1) | copy-start | bytes 7077892
  129.9 8.5 %copy-start.18 = (f32[1024,128]{1,0:T(8,128)S(1)}, f32[1024,128]{1,0:T(8,128)}, u32[]{:S(2)}) copy-start(f32[1024,128]{1,0:T(8,128)} %fusion.77) | copy-start | bytes 1572868
  134.9 4.7 %copy-start.17 = (f32[1024,128]{1,0:T(8,128)S(1)}, f32[1024,128]{1,0:T(8,128)}, u32[]{:S(2)}) copy-start(f32[1024,128]{1,0:T(8,128)} %fusion.81) | copy-start | bytes 1572868
  136.4 74.3 %collective-permute-start.7 = (bf16[256,128]{1,0:T(8,128)(2,1)}, bf16[256,128]{1,0:T(8,128)(2,1)}, u32[]{:S(2)}, u32[]{:S(2)}) collective-permute-start(bf16[256,128]{1,0:T(8,128)(2,1)} %fusion.39), channel_id=1, source_target_pairs={{0,8},{8,16},{16,24},{24,32},{32,40},{40,48},{48,56},{56,64},{64,7... | collective-permute-start | bytes 196616 | tf_op jit(solution)/shard_map/ppermute | solution.py:16
  140.1 9.0 %copy-start.3 = (bf16[512,2304]{1,0:T(8,128)(2,1)S(1)}, bf16[512,2304]{1,0:T(8,128)(2,1)}, u32[]{:S(2)}) copy-start(bf16[512,2304]{1,0:T(8,128)(2,1)} %get-tuple-element.34) | copy-start | bytes 7077892
  141.9 68.9 %collective-permute-start.6 = (f32[1024,128]{1,0:T(8,128)}, f32[1024,128]{1,0:T(8,128)}, u32[]{:S(2)}, u32[]{:S(2)}) collective-permute-start(f32[1024,128]{1,0:T(8,128)} %convolution_add_fusion), channel_id=1, source_target_pairs={{8,0},{16,8},{24,16},{32,24},{40,32},{48,40},{56,48},{64,56},{72,6... | collective-permute-start | bytes 1572872 | tf_op jit(solution)/shard_map/ppermute | solution.py:16
  162.0 11.5 %copy-start.4 = (bf16[512,2304]{1,0:T(8,128)(2,1)}, bf16[512,2304]{1,0:T(8,128)(2,1)S(1)}, u32[]{:S(2)}) copy-start(bf16[512,2304]{1,0:T(8,128)(2,1)S(1)} %get-tuple-element.36) | copy-start | bytes 7077892
  162.0 7.3 %copy-start.19 = (f32[1024,128]{1,0:T(8,128)S(1)}, f32[1024,128]{1,0:T(8,128)}, u32[]{:S(2)}) copy-start(f32[1024,128]{1,0:T(8,128)} %fusion.59) | copy-start | bytes 1572868
  165.7 4.0 %copy-start.5 = (bf16[512,2304]{1,0:T(8,128)(2,1)S(1)}, bf16[512,2304]{1,0:T(8,128)(2,1)}, u32[]{:S(2)}) copy-start(bf16[512,2304]{1,0:T(8,128)(2,1)} %get-tuple-element.35) | copy-start | bytes 7077892
  167.2 3.9 %copy-start.13 = (bf16[512,2304]{1,0:T(8,128)(2,1)S(1)}, bf16[512,2304]{1,0:T(8,128)(2,1)}, u32[]{:S(2)}) copy-start(bf16[512,2304]{1,0:T(8,128)(2,1)} %get-tuple-element.33) | copy-start | bytes 7077892
  167.2 49.4 %collective-permute-start.5 = (bf16[256,128]{1,0:T(8,128)(2,1)}, bf16[256,128]{1,0:T(8,128)(2,1)}, u32[]{:S(2)}, u32[]{:S(2)}) collective-permute-start(bf16[256,128]{1,0:T(8,128)(2,1)} %fusion.38), channel_id=1, source_target_pairs={{0,8},{8,16},{16,24},{24,32},{32,40},{40,48},{48,56},{56,64},{64,7... | collective-permute-start | bytes 196616 | tf_op jit(solution)/shard_map/ppermute | solution.py:16
  169.7 2.2 copy-start.12
  169.7 2.2 copy-start.15
  171.0 1.4 copy-start.16
  174.0 15.2 %copy-start.23 = (bf16[512,128]{0,1:T(8,128)(2,1)S(1)}, bf16[512,128]{0,1:T(8,128)(2,1)}, u32[]{:S(2)}) copy-start(bf16[512,128]{0,1:T(8,128)(2,1)} %copy-done.22) | copy-start | bytes 393220
  174.9 16.2 %copy-start.10 = (bf16[1024,256]{0,1:T(8,128)(2,1)S(1)}, bf16[1024,256]{0,1:T(8,128)(2,1)}, u32[]{:S(2)}) copy-start(bf16[1024,256]{0,1:T(8,128)(2,1)} %copy-done.8) | copy-start | bytes 1572868
  174.9 18.7 %all-to-all-start.5 = ((bf16[8,128,256]{1,2,0:T(8,128)(2,1)}), bf16[8,128,256]{1,2,0:T(8,128)(2,1)}, u32[]{:S(2)}, u32[]{:S(2)}) async-start(bf16[8,128,256]{1,2,0:T(8,128)(2,1)} %copy_bitcast_fusion.1), calls=%async_computation.5 | async-start | bytes 1048576 | tf_op jit(solution)/shard_map/all_to_all | solution.py:133
  179.2 11.9 %copy-start.14 = (f32[1024,128]{1,0:T(8,128)S(1)}, f32[1024,128]{1,0:T(8,128)}, u32[]{:S(2)}) copy-start(f32[1024,128]{1,0:T(8,128)} %convolution_add_fusion.5) | copy-start | bytes 1572868
  181.9 34.7 %collective-permute-start.4 = (f32[1024,128]{1,0:T(8,128)}, f32[1024,128]{1,0:T(8,128)}, u32[]{:S(2)}, u32[]{:S(2)}) collective-permute-start(f32[1024,128]{1,0:T(8,128)} %convolution_add_fusion.6), channel_id=1, source_target_pairs={{8,0},{16,8},{24,16},{32,24},{40,32},{48,40},{56,48},{64,56},{72,6... | collective-permute-start | bytes 1572872 | tf_op jit(solution)/shard_map/ppermute | solution.py:16
  193.6 15.1 %all-to-all-start.3 = ((bf16[8,128,256]{1,2,0:T(8,128)(2,1)}), bf16[8,128,256]{1,2,0:T(8,128)(2,1)}, u32[]{:S(2)}, u32[]{:S(2)}) async-start(bf16[8,128,256]{1,2,0:T(8,128)(2,1)} %copy_bitcast_fusion.2), calls=%async_computation.3 | async-start | bytes 1048576 | tf_op jit(solution)/shard_map/all_to_all | solution.py:132
  213.2 10.9 %all-to-all-start.7 = ((bf16[8,128,128]{2,1,0:T(8,128)(2,1)}), bf16[8,128,128]{2,1,0:T(8,128)(2,1)S(1)}, u32[]{:S(2)}, u32[]{:S(2)}) async-start(bf16[8,128,128]{2,1,0:T(8,128)(2,1)} %bitcast.143), calls=%async_computation.7 | async-start | bytes 524288 | tf_op jit(solution)/shard_map/all_to_all | solution.py:137
  224.0 10.9 %all-to-all-start.6 = ((bf16[8,128,128]{2,1,0:T(8,128)(2,1)}), bf16[8,128,128]{2,1,0:T(8,128)(2,1)S(1)}, u32[]{:S(2)}, u32[]{:S(2)}) async-start(bf16[8,128,128]{2,1,0:T(8,128)(2,1)} %bitcast.17), calls=%async_computation.6 | async-start | bytes 524288 | tf_op jit(solution)/shard_map/all_to_all | solution.py:134
where the time goes:
time: 238 us; the launch traced here: 236 us
  matrix products  90.7 us (38%)
  starting transfers between devices  65.3 us (27%)
  waiting for transfers between devices  32.2 us (14%)
  other arithmetic  30.3 us (13%)
  local copies, waits for them, and re-layouts  15.7 us (7%)
    dot_general x72, matrix products, product(): lax.dot_general(left, right, (dims, ((), ())), preferred_element_type=jnp...  90.7 us
    ppermute x8, starting transfers between devices, shifted(): return lax.ppermute(value, axis, pairs)  33.4 us
    convert_element_type x2, other arithmetic, local(): (query_scale * probs * (grad_probs - delta)).astype(jnp.bfloat16)  13.6 us
    unnamed x70, local copies, waits for them, and re-layouts  9.88 us
    reduce_max x1, other arithmetic, local(): top = jnp.max(scores, axis=-1, keepdims=True)  7.43 us
    all_to_all x1, waiting for transfers between devices, local(): lax.all_to_all(grad_key_sum.astype(jnp.bfloat16), 'head', split_axis=0, c...  6.71 us
    all_to_all x1, waiting for transfers between devices, local(): lax.all_to_all(value_rows, 'head', split_axis=1, concat_axis=0, tiled=True)  6.44 us
    all_to_all x1, waiting for transfers between devices, local(): lax.all_to_all(key_rows, 'head', split_axis=1, concat_axis=0, tiled=True)  5.75 us
  transfers between devices with their start and end apart: 16, of which 6 were waited for; matrix products, arithmetic and copies ran while one was open for 44% of the time, Pallas kernels for 0%

commit v1 on v0

v1 whole, which is shorter than its diff:
```python
import jax
import jax.numpy as jnp
from jax import lax
from jax.experimental import pallas as pl
from jax.experimental.pallas import tpu as pltpu
from jax.sharding import PartitionSpec as P

HD = 128
BLK = 1024
PIECE = 128
TILE = 256
SCALE = 168.0 ** (-0.5)
SCALE_LOG2 = SCALE * 1.4426950408889634
MASKED = -1e30
MESH = pl.DeviceIdType.MESH
f32 = jnp.float32
bf16 = jnp.bfloat16


def matmul(left, right):
    return lax.dot_general(left, right, (((1,), (0,)), ((), ())), preferred_element_type=f32)


def kernel(
    q_hbm, k_hbm, v_hbm, g_hbm, lower_ref, upper_ref,
    o_hbm, gq_hbm, gk_hbm, gv_hbm,
    q_buf, g_buf, k_win, v_win, kt_win, vt_win, p_buf, dk_acc, dv_acc,
    o_buf, gq_buf, ret_send, ret_recv, own_buf,
    in_ssem, in_rsem, fwd_ssem, fwd_rsem, ahead_ssem, ahead_rsem,
    out_ssem, out_rsem, ret_ssem, ret_rsem, own_ssem, own_rsem,
):
    n_ctx = lax.axis_size("ctx")
    n = lax.axis_size("head")
    c = lax.axis_index("ctx")
    h = lax.axis_index("head")
    after = lax.rem(c + 1, n_ctx)
    before = lax.rem(c + n_ctx - 1, n_ctx)

    barrier = pltpu.get_barrier_semaphore()

    @pl.loop(1, n)
    def _(r):
        pl.semaphore_signal(barrier, inc=1, device_id=(c, lax.rem(h + r, n)), device_id_type=MESH)

    pl.semaphore_signal(barrier, inc=1, device_id=(after, h), device_id_type=MESH)
    pl.semaphore_signal(barrier, inc=1, device_id=(before, h), device_id_type=MESH)
    pl.semaphore_wait(barrier, n + 1)

    def in_src(stream, target):
        if stream < 2:
            return (k_hbm, v_hbm)[stream].at[:, pl.ds(pl.multiple_of(target * HD, HD), HD)]
        head = (stream - 2) // 2
        cols = pl.ds(pl.multiple_of(target * 2 * HD + head * HD, HD), HD)
        return (q_hbm, g_hbm)[stream % 2].at[:, cols]

    def in_dst(stream, source):
        if stream < 2:
            return (k_win, v_win)[stream].at[8 + source]
        return (q_buf, g_buf)[stream % 2].at[(stream - 2) // 2, source]

    def send_in(streams):
        for stream in streams:
            pltpu.make_async_copy(
                in_src(stream, h), in_dst(stream, h), in_rsem.at[stream, h]
            ).start()

        @pl.loop(1, n)
        def _(r):
            target = lax.rem(h + r, n)
            for stream in streams:
                pltpu.make_async_remote_copy(
                    src_ref=in_src(stream, target),
                    dst_ref=in_dst(stream, h),
                    send_sem=in_ssem.at[stream, target],
                    recv_sem=in_rsem.at[stream, h],
                    device_id=(c, target),
                    device_id_type=MESH,
                ).start()

    def wait_in(stream, source):
        dst = in_dst(stream, source)
        pltpu.make_async_copy(dst, dst, in_rsem.at[stream, source]).wait()

    def forward(side, piece):
        win = (k_win, v_win)[side]
        return pltpu.make_async_remote_copy(
            src_ref=win.at[8 + piece],
            dst_ref=win.at[piece],
            send_sem=fwd_ssem.at[side, piece],
            recv_sem=fwd_rsem.at[side, piece],
            device_id=(after, h),
            device_id_type=MESH,
        )

    def ahead(side, piece):
        win = (k_win, v_win)[side]
        return pltpu.make_async_remote_copy(
            src_ref=win.at[8 + piece],
            dst_ref=win.at[16 + piece],
            send_sem=ahead_ssem.at[side, piece],
            recv_sem=ahead_rsem.at[side, piece],
            device_id=(before, h),
            device_id_type=MESH,
        )

    send_in((0, 1))
    send_in((2, 3))

    @pl.loop(0, n)
    def _(r):
        source = lax.rem(h + n - r, n)
        for side in range(2):
            wait_in(side, source)
            forward(side, source).start()

        @pl.when(source < 2)
        def _():
            for side in range(2):
                ahead(side, source).start()

    send_in((4, 5))

    dk_acc[...] = jnp.zeros_like(dk_acc)
    dv_acc[...] = jnp.zeros_like(dv_acc)

    @pl.loop(0, 8)
    def _(piece):
        for side in range(2):
            forward(side, piece).wait_recv()

    @pl.loop(0, 2)
    def _(piece):
        for side in range(2):
            ahead(side, piece).wait_recv()

    @pl.loop(0, 9)
    def _(tile):
        rows = pl.ds(2 * tile, 2)
        kt_win[tile] = k_win[rows].reshape(TILE, HD).T
        vt_win[tile] = v_win[rows].reshape(TILE, HD).T

    place = lax.broadcasted_iota(jnp.int32, (TILE, TILE), 0)

    def block(head, i, tiles):
        rows = pl.ds(2 * i, 2)
        q = q_buf[head, rows].reshape(TILE, HD)
        g = g_buf[head, rows].reshape(TILE, HD)
        qt = q.T
        gt = g.T
        first = (c - 1) * BLK + i * TILE
        lower = lower_ref[i] - first
        upper = upper_ref[i] - first
        top = None
        for t in range(tiles):
            s = matmul(k_win[pl.ds(2 * (i + t), 2)].reshape(TILE, HD), qt) * SCALE_LOG2
            allowed = place >= lower - t * TILE
            if t >= 4:
                allowed = allowed & (place <= upper - t * TILE)
            s = jnp.where(allowed, s, MASKED)
            p_buf[t] = s
            most = jnp.max(s, axis=0, keepdims=True)
            top = most if top is None else jnp.maximum(top, most)
        total = None
        out = None
        for t in range(tiles):
            p = jnp.exp2(p_buf[t] - top)
            p_buf[t] = p
            part = jnp.sum(p, axis=0, keepdims=True)
            term = matmul(vt_win[i + t], p.astype(bf16))
            total = part if total is None else total + part
            out = term if out is None else out + term
        share = 1.0 / total
        out = (out * share).astype(bf16)
        delta = jnp.sum(gt.astype(f32) * out.astype(f32), axis=0, keepdims=True)
        o_buf[head, rows] = out.T.reshape(2, PIECE, HD)
        scaled = share * SCALE
        offset = delta * scaled
        grad_q = None
        for t in range(tiles):
            p = p_buf[t]
            dv_acc[i + t] += matmul((p * share).astype(bf16), g)
            dp = matmul(v_win[pl.ds(2 * (i + t), 2)].reshape(TILE, HD), gt)
            ds = (p * (dp * scaled - offset)).astype(bf16)
            dk_acc[i + t] += matmul(ds, q)
            term = matmul(kt_win[i + t], ds)
            grad_q = term if grad_q is None else grad_q + term
        gq_buf[head, rows] = grad_q.astype(bf16).T.reshape(2, PIECE, HD)

    def out_src(kind, head, target):
        return (o_buf, gq_buf)[kind].at[head, target]

    def out_dst(kind, head, source):
        cols = pl.ds(pl.multiple_of(source * 2 * HD + head * HD, HD), HD)
        return (o_hbm, gq_hbm)[kind].at[:, cols]

    def send_out(kind, head, target):
        @pl.when(target == h)
        def _():
            pltpu.make_async_copy(
                out_src(kind, head, target), out_dst(kind, head, h), out_rsem.at[kind, head, h]
            ).start()

        @pl.when(target != h)
        def _():
            pltpu.make_async_remote_copy(
                src_ref=out_src(kind, head, target),
                dst_ref=out_dst(kind, head, h),
                send_sem=out_ssem.at[kind, head, target],
                recv_sem=out_rsem.at[kind, head, h],
                device_id=(c, target),
                device_id_type=MESH,
            ).start()

    def give_back(side, slot):
        return pltpu.make_async_remote_copy(
            src_ref=ret_send.at[side, slot],
            dst_ref=ret_recv.at[side, slot],
            send_sem=ret_ssem.at[side, slot],
            recv_sem=ret_rsem.at[side, slot],
            device_id=(jnp.where(slot == 4, after, before), h),
            device_id_type=MESH,
        )

    for head in range(2):

        @pl.loop(0, n)
        def _(source):
            for kind in range(2):
                wait_in(2 + 2 * head + kind, source)

        @pl.loop(0, 4)
        def _(i):
            @pl.when(i < 3)
            def _():
                block(head, i, 5)

            @pl.when(i == 3)
            def _():
                block(head, i, 6)

            for kind in range(2):
                for part in range(2):
                    send_out(kind, head, 2 * i + part)
            if head == 1:
                ret_send[0, i] = dk_acc[i].astype(bf16)
                ret_send[1, i] = dv_acc[i].astype(bf16)
                for side in range(2):
                    give_back(side, i).start()

    ret_send[0, 4] = dk_acc[8].astype(bf16)
    ret_send[1, 4] = dv_acc[8].astype(bf16)
    for side in range(2):
        give_back(side, 4).start()

    def own_dst(side, source):
        return (gk_hbm, gv_hbm)[side].at[:, pl.ds(pl.multiple_of(source * HD, HD), HD)]

    def send_own(side, target):
        @pl.when(target == h)
        def _():
            pltpu.make_async_copy(
                own_buf.at[side, target], own_dst(side, h), own_rsem.at[side, h]
            ).start()

        @pl.when(target != h)
        def _():
            pltpu.make_async_remote_copy(
                src_ref=own_buf.at[side, target],
                dst_ref=own_dst(side, h),
                send_sem=own_ssem.at[side, target],
                recv_sem=own_rsem.at[side, h],
                device_id=(c, target),
                device_id_type=MESH,
            ).start()

    @pl.loop(0, 4)
    def _(tile):
        for side in range(2):
            give_back(side, tile).wait_recv()
            acc = (dk_acc, dv_acc)[side]

            @pl.when(tile == 0)
            def _():
                give_back(side, 4).wait_recv()
                acc[4] += ret_recv[side, 4].astype(f32)

            total = acc[4 + tile] + ret_recv[side, tile].astype(f32)
            own_buf[side, pl.ds(2 * tile, 2)] = total.astype(bf16).reshape(2, PIECE, HD)
            for part in range(2):
                send_own(side, 2 * tile + part)

    @pl.loop(0, n)
    def _(other):
        for kind in range(2):
            for head in range(2):
                dst = out_dst(kind, head, other)
                pltpu.make_async_copy(dst, dst, out_rsem.at[kind, head, other]).wait()
            dst = own_dst(kind, other)
            pltpu.make_async_copy(dst, dst, own_rsem.at[kind, other]).wait()
            forward(kind, other).wait_send()

        @pl.when(other != h)
        def _():
            for stream in range(6):
                src = in_src(stream, other)
                pltpu.make_async_copy(src, src, in_ssem.at[stream, other]).wait()
            for kind in range(2):
                for head in range(2):
                    src = out_src(kind, head, other)
                    pltpu.make_async_copy(src, src, out_ssem.at[kind, head, other]).wait()
                src = own_buf.at[kind, other]
                pltpu.make_async_copy(src, src, own_ssem.at[kind, other]).wait()

    @pl.loop(0, 5)
    def _(slot):
        for side in range(2):
            give_back(side, slot).wait_send()

    @pl.loop(0, 2)
    def _(piece):
        for side in range(2):
            ahead(side, piece).wait_send()


def local(queries, key_rows, value_rows, grad_out, doc_start, reach_end):
    dma = pltpu.SemaphoreType.DMA
    hbm = pl.BlockSpec(memory_space=pltpu.HBM)
    vmem = pl.BlockSpec(memory_space=pltpu.VMEM)
    return pl.pallas_call(
        kernel,
        out_shape=[
            jax.ShapeDtypeStruct(queries.shape, bf16),
            jax.ShapeDtypeStruct(queries.shape, bf16),
            jax.ShapeDtypeStruct(key_rows.shape, bf16),
            jax.ShapeDtypeStruct(key_rows.shape, bf16),
        ],
        in_specs=[hbm, hbm, hbm, hbm, vmem, vmem],
        out_specs=[hbm, hbm, hbm, hbm],
        scratch_shapes=[
            pltpu.VMEM((2, 8, PIECE, HD), bf16),
            pltpu.VMEM((2, 8, PIECE, HD), bf16),
            pltpu.VMEM((18, PIECE, HD), bf16),
            pltpu.VMEM((18, PIECE, HD), bf16),
            pltpu.VMEM((9, HD, TILE), bf16),
            pltpu.VMEM((9, HD, TILE), bf16),
            pltpu.VMEM((6, TILE, TILE), f32),
            pltpu.VMEM((9, TILE, HD), f32),
            pltpu.VMEM((9, TILE, HD), f32),
            pltpu.VMEM((2, 8, PIECE, HD), bf16),
            pltpu.VMEM((2, 8, PIECE, HD), bf16),
            pltpu.VMEM((2, 5, TILE, HD), bf16),
            pltpu.VMEM((2, 5, TILE, HD), bf16),
            pltpu.VMEM((2, 8, PIECE, HD), bf16),
            dma((6, 8)),
            dma((6, 8)),
            dma((2, 8)),
            dma((2, 8)),
            dma((2, 2)),
            dma((2, 2)),
            dma((2, 2, 8)),
            dma((2, 2, 8)),
            dma((2, 5)),
            dma((2, 5)),
            dma((2, 8)),
            dma((2, 8)),
        ],
        compiler_params=pltpu.CompilerParams(
            collective_id=0, has_side_effects=True, vmem_limit_bytes=40 * 1024 * 1024
        ),
    )(
        queries, key_rows, value_rows, grad_out,
        doc_start.reshape(4, 1, TILE), reach_end.reshape(4, 1, TILE),
    )


def solution(mesh):
    rows = P(("ctx", "head"), None)
    return jax.shard_map(
        local,
        mesh=mesh,
        in_specs=(rows, rows, rows, rows, P("ctx"), P("ctx")),
        out_specs=(rows, rows, rows, rows),
        check_vma=False,
    )
```

time: 238 us -> 72 us (0.30)
  the two profiles are of different devices: /device:TPU:128 before, /device:TPU:7 now
where the time goes in v1:
time: 72 us; the launch traced here: 71.6 us
  Pallas kernels  62.6 us (87%)
  local copies, waits for them, and re-layouts  8.34 us (12%)
    pallas_call x1, Pallas kernels, local(): pl.pallas_call(kernel, out_shape=[jax.ShapeDtypeStruct(queries.shape, bf1...  62.6 us
    unnamed x16, local copies, waits for them, and re-layouts  8.34 us

profile of v1, /device:TPU:7, one launch (start us, length us, event | category | flops | bytes accessed | tf_op | source)
XLA Modules:
  0.0 71.6 jit_solution(12173352361654670292)
XLA Ops:
  0.6 0.0 copy-start
  0.6 1.0 %copy-done = bf16[128,2048]{1,0:T(8,128)(2,1)S(1)} copy-done((bf16[128,2048]{1,0:T(8,128)(2,1)S(1)}, bf16[128,2048]{1,0:T(8,128)(2,1)}, u32[]{:S(2)}) %copy-start) | copy-done | bytes 524312
  1.7 0.0 copy-start.1
  1.7 1.0 %copy-done.1 = bf16[128,2048]{1,0:T(8,128)(2,1)S(1)} copy-done((bf16[128,2048]{1,0:T(8,128)(2,1)S(1)}, bf16[128,2048]{1,0:T(8,128)(2,1)}, u32[]{:S(2)}) %copy-start.1) | copy-done | bytes 524312
  2.7 0.0 copy-start.2
  2.7 0.9 %copy-done.2 = bf16[128,1024]{1,0:T(8,128)(2,1)S(1)} copy-done((bf16[128,1024]{1,0:T(8,128)(2,1)S(1)}, bf16[128,1024]{1,0:T(8,128)(2,1)}, u32[]{:S(2)}) %copy-start.2) | copy-done | bytes 262168
  3.7 0.0 copy-start.3
  3.7 0.9 %copy-done.3 = bf16[128,1024]{1,0:T(8,128)(2,1)S(1)} copy-done((bf16[128,1024]{1,0:T(8,128)(2,1)S(1)}, bf16[128,1024]{1,0:T(8,128)(2,1)}, u32[]{:S(2)}) %copy-start.3) | copy-done | bytes 262168
  4.6 0.0 copy-start.4
  4.6 0.7 copy-done.4
  5.3 0.0 copy-start.5
  5.3 0.7 copy-done.5
  6.0 62.6 %shard_map.93 = (bf16[128,2048]{1,0:T(8,128)(2,1)S(1)}, bf16[128,2048]{1,0:T(8,128)(2,1)S(1)}, bf16[128,1024]{1,0:T(8,128)(2,1)S(1)}, bf16[128,1024]{1,0:T(8,128)(2,1)S(1)}) custom-call(bf16[128,2048]{1,0:T(8,128)(2,1)S(1)} %copy-done, bf16[128,1024]{1,0:T(8,128)(2,1)S(1)} %copy-done.2, bf16[128,1024]{1,0:T(8,128)(2,1)S(1)} %copy-done.3, ...), custom_call_target="tpu_custom_call" | custom-call | tf_op jit(solution)/shard_map/pallas_call | solution.py:329
  68.6 0.8 %copy.14 = bf16[128,2048]{1,0:T(8,128)(2,1)} copy(bf16[128,2048]{1,0:T(8,128)(2,1)S(1)} %get-tuple-element.8) | data formatting | bytes 1048576
  69.4 0.8 %copy.15 = bf16[128,2048]{1,0:T(8,128)(2,1)} copy(bf16[128,2048]{1,0:T(8,128)(2,1)S(1)} %get-tuple-element.9) | data formatting | bytes 1048576
  70.2 0.7 copy.16
  70.9 0.7 copy.17
Async XLA Ops:
  0.6 1.0 %copy-start = (bf16[128,2048]{1,0:T(8,128)(2,1)S(1)}, bf16[128,2048]{1,0:T(8,128)(2,1)}, u32[]{:S(2)}) copy-start(bf16[128,2048]{1,0:T(8,128)(2,1)} %q_hbm.1) | copy-start | bytes 1572868
  1.7 1.0 %copy-start.1 = (bf16[128,2048]{1,0:T(8,128)(2,1)S(1)}, bf16[128,2048]{1,0:T(8,128)(2,1)}, u32[]{:S(2)}) copy-start(bf16[128,2048]{1,0:T(8,128)(2,1)} %g_hbm.1) | copy-start | bytes 1572868
  2.7 0.9 %copy-start.2 = (bf16[128,1024]{1,0:T(8,128)(2,1)S(1)}, bf16[128,1024]{1,0:T(8,128)(2,1)}, u32[]{:S(2)}) copy-start(bf16[128,1024]{1,0:T(8,128)(2,1)} %k_hbm.1) | copy-start | bytes 786436
  3.7 0.9 %copy-start.3 = (bf16[128,1024]{1,0:T(8,128)(2,1)S(1)}, bf16[128,1024]{1,0:T(8,128)(2,1)}, u32[]{:S(2)}) copy-start(bf16[128,1024]{1,0:T(8,128)(2,1)} %v_hbm.1) | copy-start | bytes 786436
  4.6 0.7 copy-start.4
  5.3 0.7 copy-start.5

commit v2 on v1

--- a/solution.py
+++ b/solution.py
@@ -9,6 +9,7 @@
 BLK = 1024
 PIECE = 128
 TILE = 256
+WINDOW = 2304
 SCALE = 168.0 ** (-0.5)
 SCALE_LOG2 = SCALE * 1.4426950408889634
 MASKED = -1e30
@@ -22,11 +23,12 @@
 
 
 def kernel(
-    q_hbm, k_hbm, v_hbm, g_hbm, lower_ref, upper_ref,
+    q_hbm, k_hbm, v_hbm, g_hbm, lower_hbm, upper_hbm,
     o_hbm, gq_hbm, gk_hbm, gv_hbm,
-    q_buf, g_buf, k_win, v_win, kt_win, vt_win, p_buf, dk_acc, dv_acc,
+    lower_ref, upper_ref, q_buf, g_buf, k_win, v_win, kt_win, vt_win, s_buf, p_buf, ds_buf,
+    gt_buf, gs_buf, qs_buf, delta_buf, scaled_buf, dk_acc, dv_acc,
     o_buf, gq_buf, ret_send, ret_recv, own_buf,
-    in_ssem, in_rsem, fwd_ssem, fwd_rsem, ahead_ssem, ahead_rsem,
+    mark_sem, in_ssem, in_rsem, fwd_ssem, fwd_rsem, ahead_ssem, ahead_rsem,
     out_ssem, out_rsem, ret_ssem, ret_rsem, own_ssem, own_rsem,
 ):
     n_ctx = lax.axis_size("ctx")
@@ -103,88 +105,98 @@
             device_id_type=MESH,
         )
 
+    marks = [pltpu.make_async_copy(src, dst, mark_sem.at[k]) for k, (src, dst) in enumerate(
+        ((lower_hbm, lower_ref), (upper_hbm, upper_ref)))]
+    for mark in marks:
+        mark.start()
     send_in((0, 1))
     send_in((2, 3))
-
-    @pl.loop(0, n)
-    def _(r):
-        source = lax.rem(h + n - r, n)
-        for side in range(2):
-            wait_in(side, source)
-            forward(side, source).start()
-
-        @pl.when(source < 2)
-        def _():
-            for side in range(2):
-                ahead(side, source).start()
-
+    for piece in (7, 6, 0, 1, 5, 4, 3, 2):
+        for side in range(2):
+            wait_in(side, piece)
+            if piece >= 2:
+                forward(side, piece).start()
+            else:
+                ahead(side, piece).start()
+    for piece in (1, 0):
+        for side in range(2):
+            forward(side, piece).start()
     send_in((4, 5))
 
+    for mark in marks:
+        mark.wait()
     dk_acc[...] = jnp.zeros_like(dk_acc)
     dv_acc[...] = jnp.zeros_like(dv_acc)
 
-    @pl.loop(0, 8)
-    def _(piece):
-        for side in range(2):
-            forward(side, piece).wait_recv()
-
-    @pl.loop(0, 2)
-    def _(piece):
-        for side in range(2):
-            ahead(side, piece).wait_recv()
-
-    @pl.loop(0, 9)
-    def _(tile):
-        rows = pl.ds(2 * tile, 2)
-        kt_win[tile] = k_win[rows].reshape(TILE, HD).T
-        vt_win[tile] = v_win[rows].reshape(TILE, HD).T
+    def keys(tile):
+        return k_win[2 * tile : 2 * tile + 2].reshape(TILE, HD)
+
+    def values(tile):
+        return v_win[2 * tile : 2 * tile + 2].reshape(TILE, HD)
+
+    def turn(tile):
+        rows = pl.ds(tile * TILE, TILE)
+        kt_win[:, rows] = keys(tile).T
+        vt_win[:, rows] = values(tile).T
 
     place = lax.broadcasted_iota(jnp.int32, (TILE, TILE), 0)
 
-    def block(head, i, tiles):
+    def forward_block(head, i):
+        tiles = 6 if i == 3 else 5
         rows = pl.ds(2 * i, 2)
+        lanes = pl.ds(i * TILE, TILE)
+        window = pl.ds(i * TILE, tiles * TILE)
         q = q_buf[head, rows].reshape(TILE, HD)
         g = g_buf[head, rows].reshape(TILE, HD)
         qt = q.T
         gt = g.T
+        gt_buf[:, lanes] = gt
         first = (c - 1) * BLK + i * TILE
         lower = lower_ref[i] - first
         upper = upper_ref[i] - first
         top = None
         for t in range(tiles):
-            s = matmul(k_win[pl.ds(2 * (i + t), 2)].reshape(TILE, HD), qt) * SCALE_LOG2
+            s = matmul(keys(i + t), qt) * SCALE_LOG2
             allowed = place >= lower - t * TILE
             if t >= 4:
                 allowed = allowed & (place <= upper - t * TILE)
             s = jnp.where(allowed, s, MASKED)
-            p_buf[t] = s
+            s_buf[t] = s
             most = jnp.max(s, axis=0, keepdims=True)
             top = most if top is None else jnp.maximum(top, most)
         total = None
-        out = None
         for t in range(tiles):
-            p = jnp.exp2(p_buf[t] - top)
-            p_buf[t] = p
+            p = jnp.exp2(s_buf[t] - top)
+            p_buf[pl.ds((i + t) * TILE, TILE), lanes] = p.astype(bf16)
             part = jnp.sum(p, axis=0, keepdims=True)
-            term = matmul(vt_win[i + t], p.astype(bf16))
             total = part if total is None else total + part
-            out = term if out is None else out + term
         share = 1.0 / total
-        out = (out * share).astype(bf16)
-        delta = jnp.sum(gt.astype(f32) * out.astype(f32), axis=0, keepdims=True)
+        out = (matmul(vt_win[:, window], p_buf[window, lanes]) * share).astype(bf16)
         o_buf[head, rows] = out.T.reshape(2, PIECE, HD)
+        gt = gt.astype(f32)
+        delta_buf[i] = jnp.sum(gt * out.astype(f32), axis=0, keepdims=True)
         scaled = share * SCALE
-        offset = delta * scaled
-        grad_q = None
-        for t in range(tiles):
-            p = p_buf[t]
-            dv_acc[i + t] += matmul((p * share).astype(bf16), g)
-            dp = matmul(v_win[pl.ds(2 * (i + t), 2)].reshape(TILE, HD), gt)
-            ds = (p * (dp * scaled - offset)).astype(bf16)
-            dk_acc[i + t] += matmul(ds, q)
-            term = matmul(kt_win[i + t], ds)
-            grad_q = term if grad_q is None else grad_q + term
-        gq_buf[head, rows] = grad_q.astype(bf16).T.reshape(2, PIECE, HD)
+        scaled_buf[i] = scaled
+        gs_buf[lanes] = (gt * share).astype(bf16).T
+        qs_buf[lanes] = (qt.astype(f32) * scaled).astype(bf16).T
+
+    def backward_tile(tile):
+        blocks = range(max(0, tile - 4), 1 + min(3, tile)) if tile < 8 else range(3, 4)
+        rows = pl.ds(tile * TILE, TILE)
+        span = pl.ds(blocks[0] * TILE, len(blocks) * TILE)
+        v = values(tile)
+        dv_acc[tile] += matmul(p_buf[rows, span], gs_buf[span])
+        for i in blocks:
+            lanes = pl.ds(i * TILE, TILE)
+            dp = matmul(v, gt_buf[:, lanes])
+            ds_buf[rows, lanes] = p_buf[rows, lanes] * (dp - delta_buf[i]).astype(bf16)
+        dk_acc[tile] += matmul(ds_buf[rows, span], qs_buf[span])
+
+    def grad_queries(head, i):
+        lanes = pl.ds(i * TILE, TILE)
+        window = pl.ds(i * TILE, (6 if i == 3 else 5) * TILE)
+        grad = matmul(kt_win[:, window], ds_buf[window, lanes]) * scaled_buf[i]
+        gq_buf[head, pl.ds(2 * i, 2)] = grad.astype(bf16).T.reshape(2, PIECE, HD)
 
     def out_src(kind, head, target):
         return (o_buf, gq_buf)[kind].at[head, target]
@@ -221,37 +233,6 @@
             device_id_type=MESH,
         )
 
-    for head in range(2):
-
-        @pl.loop(0, n)
-        def _(source):
-            for kind in range(2):
-                wait_in(2 + 2 * head + kind, source)
-
-        @pl.loop(0, 4)
-        def _(i):
-            @pl.when(i < 3)
-            def _():
-                block(head, i, 5)
-
-            @pl.when(i == 3)
-            def _():
-                block(head, i, 6)
-
-            for kind in range(2):
-                for part in range(2):
-                    send_out(kind, head, 2 * i + part)
-            if head == 1:
-                ret_send[0, i] = dk_acc[i].astype(bf16)
-                ret_send[1, i] = dv_acc[i].astype(bf16)
-                for side in range(2):
-                    give_back(side, i).start()
-
-    ret_send[0, 4] = dk_acc[8].astype(bf16)
-    ret_send[1, 4] = dv_acc[8].astype(bf16)
-    for side in range(2):
-        give_back(side, 4).start()
-
     def own_dst(side, source):
         return (gk_hbm, gv_hbm)[side].at[:, pl.ds(pl.multiple_of(source * HD, HD), HD)]
 
@@ -273,21 +254,65 @@
                 device_id_type=MESH,
             ).start()
 
-    @pl.loop(0, 4)
-    def _(tile):
+    def send_sum(tile):
         for side in range(2):
             give_back(side, tile).wait_recv()
             acc = (dk_acc, dv_acc)[side]
-
-            @pl.when(tile == 0)
-            def _():
+            total = acc[4 + tile] + ret_recv[side, tile].astype(f32)
+            if tile == 0:
                 give_back(side, 4).wait_recv()
-                acc[4] += ret_recv[side, 4].astype(f32)
-
-            total = acc[4 + tile] + ret_recv[side, tile].astype(f32)
-            own_buf[side, pl.ds(2 * tile, 2)] = total.astype(bf16).reshape(2, PIECE, HD)
+                total += ret_recv[side, 4].astype(f32)
+            own_buf[side, 2 * tile : 2 * tile + 2] = total.astype(bf16).reshape(2, PIECE, HD)
             for part in range(2):
                 send_own(side, 2 * tile + part)
+
+    def send_back(slot):
+        tile = 8 if slot == 4 else slot
+        for side in range(2):
+            ret_send[side, slot] = (dk_acc, dv_acc)[side][tile].astype(bf16)
+            give_back(side, slot).start()
+
+    @pl.loop(0, 2)
+    def _(head):
+        @pl.loop(0, n)
+        def _(source):
+            for kind in range(2):
+                dst = (q_buf, g_buf)[kind].at[head, source]
+                pltpu.make_async_copy(dst, dst, in_rsem.at[2 + 2 * head + kind, source]).wait()
+
+        for i in (3, 2, 1, 0):
+            @pl.when(head == 0)
+            def _():
+                for piece in (2 * i, 2 * i + 1):
+                    for side in range(2):
+                        forward(side, piece).wait_recv()
+                turn(i)
+                if i == 3:
+                    for piece in range(2):
+                        for side in range(2):
+                            ahead(side, piece).wait_recv()
+                    for tile in range(4, 9):
+                        turn(tile)
+
+            forward_block(head, i)
+            for part in range(2):
+                send_out(0, head, 2 * i + part)
+
+        for tile in (0, 1, 2, 3, 8, 4, 5, 6, 7):
+            backward_tile(tile)
+            if tile in (0, 1, 2, 3, 8):
+                @pl.when(head == 1)
+                def _():
+                    send_back(min(tile, 4))
+            else:
+                grad_queries(head, tile - 4)
+                for part in range(2):
+                    send_out(1, head, 2 * (tile - 4) + part)
+            if tile in (6, 7):
+                @pl.when(head == 1)
+                def _():
+                    for own in ((0, 1) if tile == 6 else (2, 3)):
+                        send_sum(own)
 
     @pl.loop(0, n)
     def _(other):
@@ -322,11 +347,18 @@
             ahead(side, piece).wait_send()
 
 
+def place_results(*refs):
+    copies = [pltpu.make_async_copy(refs[k], refs[4 + k], refs[8].at[k]) for k in range(4)]
+    for copy in copies:
+        copy.start()
+    for copy in copies:
+        copy.wait()
+
+
 def local(queries, key_rows, value_rows, grad_out, doc_start, reach_end):
     dma = pltpu.SemaphoreType.DMA
     hbm = pl.BlockSpec(memory_space=pltpu.HBM)
-    vmem = pl.BlockSpec(memory_space=pltpu.VMEM)
-    return pl.pallas_call(
+    results = pl.pallas_call(
         kernel,
         out_shape=[
             jax.ShapeDtypeStruct(queries.shape, bf16),
@@ -334,16 +366,25 @@
             jax.ShapeDtypeStruct(key_rows.shape, bf16),
             jax.ShapeDtypeStruct(key_rows.shape, bf16),
         ],
-        in_specs=[hbm, hbm, hbm, hbm, vmem, vmem],
+        in_specs=[hbm] * 6,
         out_specs=[hbm, hbm, hbm, hbm],
         scratch_shapes=[
+            pltpu.VMEM((4, 1, TILE), jnp.int32),
+            pltpu.VMEM((4, 1, TILE), jnp.int32),
             pltpu.VMEM((2, 8, PIECE, HD), bf16),
             pltpu.VMEM((2, 8, PIECE, HD), bf16),
             pltpu.VMEM((18, PIECE, HD), bf16),
             pltpu.VMEM((18, PIECE, HD), bf16),
-            pltpu.VMEM((9, HD, TILE), bf16),
-            pltpu.VMEM((9, HD, TILE), bf16),
+            pltpu.VMEM((HD, WINDOW), bf16),
+            pltpu.VMEM((HD, WINDOW), bf16),
             pltpu.VMEM((6, TILE, TILE), f32),
+            pltpu.VMEM((WINDOW, BLK), bf16),
+            pltpu.VMEM((WINDOW, BLK), bf16),
+            pltpu.VMEM((HD, BLK), bf16),
+            pltpu.VMEM((BLK, HD), bf16),
+            pltpu.VMEM((BLK, HD), bf16),
+            pltpu.VMEM((4, 1, TILE), f32),
+            pltpu.VMEM((4, 1, TILE), f32),
             pltpu.VMEM((9, TILE, HD), f32),
             pltpu.VMEM((9, TILE, HD), f32),
             pltpu.VMEM((2, 8, PIECE, HD), bf16),
@@ -351,6 +392,7 @@
             pltpu.VMEM((2, 5, TILE, HD), bf16),
             pltpu.VMEM((2, 5, TILE, HD), bf16),
             pltpu.VMEM((2, 8, PIECE, HD), bf16),
+            dma((2,)),
             dma((6, 8)),
             dma((6, 8)),
             dma((2, 8)),
@@ -365,12 +407,20 @@
             dma((2, 8)),
         ],
         compiler_params=pltpu.CompilerParams(
-            collective_id=0, has_side_effects=True, vmem_limit_bytes=40 * 1024 * 1024
+            collective_id=0, has_side_effects=True, vmem_limit_bytes=63 * 1024 * 1024
         ),
     )(
         queries, key_rows, value_rows, grad_out,
         doc_start.reshape(4, 1, TILE), reach_end.reshape(4, 1, TILE),
     )
+    return pl.pallas_call(
+        place_results,
+        out_shape=[jax.ShapeDtypeStruct(r.shape, r.dtype) for r in results],
+        in_specs=[hbm] * 4,
+        out_specs=[hbm] * 4,
+        scratch_shapes=[dma((4,))],
+        compiler_params=pltpu.CompilerParams(vmem_limit_bytes=63 * 1024 * 1024),
+    )(*results)
 
 
 def solution(mesh):

time: 72 us -> 113 us (1.57)
  Pallas kernels: 62.6 us -> 112 us
  local copies, waits for them, and re-layouts: 8.34 us -> 0 us
    pallas_call x0 -> x1, Pallas kernels: none -> 48.8 us  [local(): pl.pallas_call(place_results, out_shape=[jax.ShapeDtypeStruct(r.shape, r....]
    unnamed x16 -> x0, local copies, waits for them, and re-layouts: 8.34 us -> none
where the time goes in v2:
time: 113 us; the launch traced here: 112 us
  Pallas kernels  112 us (99%)
    pallas_call x1, Pallas kernels, local(): pl.pallas_call(kernel, out_shape=[jax.ShapeDtypeStruct(queries.shape, bf1...  63 us
    pallas_call x1, Pallas kernels, local(): pl.pallas_call(place_results, out_shape=[jax.ShapeDtypeStruct(r.shape, r....  48.8 us

profile of v2, /device:TPU:7, one launch (start us, length us, event | category | flops | bytes accessed | tf_op | source)
XLA Modules:
  0.0 112.4 jit_solution(7012149571337788465)
XLA Ops:
  0.6 63.0 %shard_map.93 = (bf16[128,2048]{1,0:T(8,128)(2,1)}, bf16[128,2048]{1,0:T(8,128)(2,1)}, bf16[128,1024]{1,0:T(8,128)(2,1)}, bf16[128,1024]{1,0:T(8,128)(2,1)}) custom-call(bf16[128,2048]{1,0:T(8,128)(2,1)} %q_hbm.1, bf16[128,1024]{1,0:T(8,128)(2,1)} %k_hbm.1, bf16[128,1024]{1,0:T(8,128)(2,1)} %v_hbm.1, bf16[128,2048]{1,0:T(8,128)(2,1)} %g_hbm.1, ...), custom_call_target="tpu_custom_call" | custom-call | tf_op jit(solution)/shard_map/pallas_call | solution.py:361
  63.6 48.8 %shard_map.94 = (bf16[128,2048]{1,0:T(8,128)(2,1)}, bf16[128,2048]{1,0:T(8,128)(2,1)}, bf16[128,1024]{1,0:T(8,128)(2,1)}, bf16[128,1024]{1,0:T(8,128)(2,1)}) custom-call(bf16[128,2048]{1,0:T(8,128)(2,1)} %get-tuple-element.8.refs_0_, bf16[128,2048]{1,0:T(8,128)(2,1)} %get-tuple-element.9.refs_1_, bf16[128,1024]{1,0:T(8,128)(2,1)} %get-tuple-element.10.refs_2_, ...), custom_call_target="tpu_custom_call" | custom-call | tf_op jit(solution)/shard_map/pallas_call | solution.py:416

commit v3 on v2

--- a/solution.py
+++ b/solution.py
@@ -28,7 +28,7 @@
     lower_ref, upper_ref, q_buf, g_buf, k_win, v_win, kt_win, vt_win, s_buf, p_buf, ds_buf,
     gt_buf, gs_buf, qs_buf, delta_buf, scaled_buf, dk_acc, dv_acc,
     o_buf, gq_buf, ret_send, ret_recv, own_buf,
-    mark_sem, in_ssem, in_rsem, fwd_ssem, fwd_rsem, ahead_ssem, ahead_rsem,
+    q_own, k_own, v_own, g_own, stage_sem, mark_sem, in_ssem, in_rsem, fwd_ssem, fwd_rsem, ahead_ssem, ahead_rsem,
     out_ssem, out_rsem, ret_ssem, ret_rsem, own_ssem, own_rsem,
 ):
     n_ctx = lax.axis_size("ctx")
@@ -38,6 +38,15 @@
     after = lax.rem(c + 1, n_ctx)
     before = lax.rem(c + n_ctx - 1, n_ctx)
 
+    stages = [
+        pltpu.make_async_copy(src, dst, stage_sem.at[k])
+        for k, (src, dst) in enumerate(
+            ((k_hbm, k_own), (v_hbm, v_own), (q_hbm, q_own), (g_hbm, g_own))
+        )
+    ]
+    for stage in stages:
+        stage.start()
+
     barrier = pltpu.get_barrier_semaphore()
 
     @pl.loop(1, n)
@@ -50,10 +59,10 @@
 
     def in_src(stream, target):
         if stream < 2:
-            return (k_hbm, v_hbm)[stream].at[:, pl.ds(pl.multiple_of(target * HD, HD), HD)]
+            return (k_own, v_own)[stream].at[:, pl.ds(pl.multiple_of(target * HD, HD), HD)]
         head = (stream - 2) // 2
         cols = pl.ds(pl.multiple_of(target * 2 * HD + head * HD, HD), HD)
-        return (q_hbm, g_hbm)[stream % 2].at[:, cols]
+        return (q_own, g_own)[stream % 2].at[:, cols]
 
     def in_dst(stream, source):
         if stream < 2:
@@ -105,11 +114,17 @@
             device_id_type=MESH,
         )
 
-    marks = [pltpu.make_async_copy(src, dst, mark_sem.at[k]) for k, (src, dst) in enumerate(
-        ((lower_hbm, lower_ref), (upper_hbm, upper_ref)))]
+    marks = [
+        pltpu.make_async_copy(src, dst, mark_sem.at[k])
+        for k, (src, dst) in enumerate(((lower_hbm, lower_ref), (upper_hbm, upper_ref)))
+    ]
     for mark in marks:
         mark.start()
+    stages[0].wait()
+    stages[1].wait()
     send_in((0, 1))
+    stages[2].wait()
+    stages[3].wait()
     send_in((2, 3))
     for piece in (7, 6, 0, 1, 5, 4, 3, 2):
         for side in range(2):
@@ -348,11 +363,16 @@
 
 
 def place_results(*refs):
-    copies = [pltpu.make_async_copy(refs[k], refs[4 + k], refs[8].at[k]) for k in range(4)]
-    for copy in copies:
-        copy.start()
-    for copy in copies:
-        copy.wait()
+    sources, places, held, sems = refs[:4], refs[4:8], refs[8:12], refs[12]
+    reads = [pltpu.make_async_copy(sources[k], held[k], sems.at[0, k]) for k in range(4)]
+    writes = [pltpu.make_async_copy(held[k], places[k], sems.at[1, k]) for k in range(4)]
+    for read in reads:
+        read.start()
+    for read, write in zip(reads, writes):
+        read.wait()
+        write.start()
+    for write in writes:
+        write.wait()
 
 
 def local(queries, key_rows, value_rows, grad_out, doc_start, reach_end):
@@ -392,6 +412,11 @@
             pltpu.VMEM((2, 5, TILE, HD), bf16),
             pltpu.VMEM((2, 5, TILE, HD), bf16),
             pltpu.VMEM((2, 8, PIECE, HD), bf16),
+            pltpu.VMEM((PIECE, 16 * HD), bf16),
+            pltpu.VMEM((PIECE, 8 * HD), bf16),
+            pltpu.VMEM((PIECE, 8 * HD), bf16),
+            pltpu.VMEM((PIECE, 16 * HD), bf16),
+            dma((4,)),
             dma((2,)),
             dma((6, 8)),
             dma((6, 8)),
@@ -418,7 +443,7 @@
         out_shape=[jax.ShapeDtypeStruct(r.shape, r.dtype) for r in results],
         in_specs=[hbm] * 4,
         out_specs=[hbm] * 4,
-        scratch_shapes=[dma((4,))],
+        scratch_shapes=[pltpu.VMEM(r.shape, r.dtype) for r in results] + [dma((2, 4))],
         compiler_params=pltpu.CompilerParams(vmem_limit_bytes=63 * 1024 * 1024),
     )(*results)
 

time: 113 us -> 65.9 us (0.58)
  Pallas kernels: 112 us -> 65.1 us
    pallas_call x1, Pallas kernels: 48.8 us -> 2.25 us  [local(): pl.pallas_call(place_results, out_shape=[jax.ShapeDtypeStruct(r.shape, r....]
where the time goes in v3:
time: 65.9 us; the launch traced here: 65.7 us
  Pallas kernels  65.1 us (99%)
    pallas_call x1, Pallas kernels, local(): pl.pallas_call(kernel, out_shape=[jax.ShapeDtypeStruct(queries.shape, bf1...  62.9 us
    pallas_call x1, Pallas kernels, local(): pl.pallas_call(place_results, out_shape=[jax.ShapeDtypeStruct(r.shape, r....  2.25 us

profile of v3, /device:TPU:7, one launch (start us, length us, event | category | flops | bytes accessed | tf_op | source)
XLA Modules:
  0.0 65.7 jit_solution(3387555725708971709)
XLA Ops:
  0.6 62.9 %shard_map.93 = (bf16[128,2048]{1,0:T(8,128)(2,1)}, bf16[128,2048]{1,0:T(8,128)(2,1)}, bf16[128,1024]{1,0:T(8,128)(2,1)}, bf16[128,1024]{1,0:T(8,128)(2,1)}) custom-call(bf16[128,2048]{1,0:T(8,128)(2,1)} %q_hbm.1, bf16[128,1024]{1,0:T(8,128)(2,1)} %k_hbm.1, bf16[128,1024]{1,0:T(8,128)(2,1)} %v_hbm.1, bf16[128,2048]{1,0:T(8,128)(2,1)} %g_hbm.1, ...), custom_call_target="tpu_custom_call" | custom-call | tf_op jit(solution)/shard_map/pallas_call | solution.py:381
  63.5 2.2 %shard_map.94 = (bf16[128,2048]{1,0:T(8,128)(2,1)}, bf16[128,2048]{1,0:T(8,128)(2,1)}, bf16[128,1024]{1,0:T(8,128)(2,1)}, bf16[128,1024]{1,0:T(8,128)(2,1)}) custom-call(bf16[128,2048]{1,0:T(8,128)(2,1)} %get-tuple-element.8.refs_0_, bf16[128,2048]{1,0:T(8,128)(2,1)} %get-tuple-element.9.refs_1_, bf16[128,1024]{1,0:T(8,128)(2,1)} %get-tuple-element.10.refs_2_, ...), custom_call_target="tpu_custom_call" | custom-call | tf_op jit(solution)/shard_map/pallas_call | solution.py:441

commit v4 on v3

--- a/solution.py
+++ b/solution.py
@@ -37,6 +37,8 @@
     h = lax.axis_index("head")
     after = lax.rem(c + 1, n_ctx)
     before = lax.rem(c + n_ctx - 1, n_ctx)
+    has_after = c < n_ctx - 1
+    has_before = c > 0
 
     stages = [
         pltpu.make_async_copy(src, dst, stage_sem.at[k])
@@ -53,9 +55,16 @@
     def _(r):
         pl.semaphore_signal(barrier, inc=1, device_id=(c, lax.rem(h + r, n)), device_id_type=MESH)
 
-    pl.semaphore_signal(barrier, inc=1, device_id=(after, h), device_id_type=MESH)
-    pl.semaphore_signal(barrier, inc=1, device_id=(before, h), device_id_type=MESH)
-    pl.semaphore_wait(barrier, n + 1)
+    @pl.when(has_after)
+    def _():
+        pl.semaphore_signal(barrier, inc=1, device_id=(after, h), device_id_type=MESH)
+
+    @pl.when(has_before)
+    def _():
+        pl.semaphore_signal(barrier, inc=1, device_id=(before, h), device_id_type=MESH)
+
+    neighbours = jnp.where(has_after, 1, 0) + jnp.where(has_before, 1, 0)
+    pl.semaphore_wait(barrier, n - 1 + neighbours)
 
     def in_src(stream, target):
         if stream < 2:
@@ -130,19 +139,32 @@
         for side in range(2):
             wait_in(side, piece)
             if piece >= 2:
+                pl.when(has_after)(forward(side, piece).start)
+            else:
+                pl.when(has_before)(ahead(side, piece).start)
+
+    @pl.when(has_after)
+    def _():
+        for piece in (1, 0):
+            for side in range(2):
                 forward(side, piece).start()
-            else:
-                ahead(side, piece).start()
-    for piece in (1, 0):
+
+    send_in((4, 5))
+
+    @pl.when(jnp.logical_not(has_before))
+    def _():
         for side in range(2):
-            forward(side, piece).start()
-    send_in((4, 5))
+            (k_win, v_win)[side][0:8] = jnp.zeros((8, PIECE, HD), bf16)
+            ret_recv[side, 4] = jnp.zeros((TILE, HD), bf16)
+
+    @pl.when(jnp.logical_not(has_after))
+    def _():
+        for side in range(2):
+            (k_win, v_win)[side][16:18] = jnp.zeros((2, PIECE, HD), bf16)
+            ret_recv[side, 0:4] = jnp.zeros((4, TILE, HD), bf16)
 
     for mark in marks:
         mark.wait()
-    dk_acc[...] = jnp.zeros_like(dk_acc)
-    dv_acc[...] = jnp.zeros_like(dv_acc)
-
     def keys(tile):
         return k_win[2 * tile : 2 * tile + 2].reshape(TILE, HD)
 
@@ -154,46 +176,53 @@
         kt_win[:, rows] = keys(tile).T
         vt_win[:, rows] = values(tile).T
 
+    for tile in range(4, 8):
+        turn(tile)
+    dk_acc[...] = jnp.zeros_like(dk_acc)
+    dv_acc[...] = jnp.zeros_like(dv_acc)
     place = lax.broadcasted_iota(jnp.int32, (TILE, TILE), 0)
 
-    def forward_block(head, i):
-        tiles = 6 if i == 3 else 5
+    def scores(head, i):
         rows = pl.ds(2 * i, 2)
-        lanes = pl.ds(i * TILE, TILE)
-        window = pl.ds(i * TILE, tiles * TILE)
-        q = q_buf[head, rows].reshape(TILE, HD)
-        g = g_buf[head, rows].reshape(TILE, HD)
-        qt = q.T
-        gt = g.T
-        gt_buf[:, lanes] = gt
+        qt = q_buf[head, rows].reshape(TILE, HD).T
+        gt_buf[:, pl.ds(i * TILE, TILE)] = g_buf[head, rows].reshape(TILE, HD).T
         first = (c - 1) * BLK + i * TILE
         lower = lower_ref[i] - first
         upper = upper_ref[i] - first
         top = None
-        for t in range(tiles):
+        for t in range(6 if i == 3 else 5):
             s = matmul(keys(i + t), qt) * SCALE_LOG2
             allowed = place >= lower - t * TILE
             if t >= 4:
                 allowed = allowed & (place <= upper - t * TILE)
             s = jnp.where(allowed, s, MASKED)
-            s_buf[t] = s
+            s_buf[i % 2, t] = s
             most = jnp.max(s, axis=0, keepdims=True)
             top = most if top is None else jnp.maximum(top, most)
+        return top
+
+    def attend(head, i, top):
+        tiles = 6 if i == 3 else 5
+        rows = pl.ds(2 * i, 2)
+        lanes = pl.ds(i * TILE, TILE)
+        window = pl.ds(i * TILE, tiles * TILE)
         total = None
         for t in range(tiles):
-            p = jnp.exp2(s_buf[t] - top)
+            p = jnp.exp2(s_buf[i % 2, t] - top)
             p_buf[pl.ds((i + t) * TILE, TILE), lanes] = p.astype(bf16)
             part = jnp.sum(p, axis=0, keepdims=True)
             total = part if total is None else total + part
         share = 1.0 / total
         out = (matmul(vt_win[:, window], p_buf[window, lanes]) * share).astype(bf16)
         o_buf[head, rows] = out.T.reshape(2, PIECE, HD)
-        gt = gt.astype(f32)
+        gt = gt_buf[:, lanes].astype(f32)
         delta_buf[i] = jnp.sum(gt * out.astype(f32), axis=0, keepdims=True)
-        scaled = share * SCALE
-        scaled_buf[i] = scaled
-        gs_buf[lanes] = (gt * share).astype(bf16).T
-        qs_buf[lanes] = (qt.astype(f32) * scaled).astype(bf16).T
+        scaled_buf[i] = share * SCALE
+        column = jnp.broadcast_to(share, (8, TILE)).T[:, :1]
+        g = g_buf[head, rows].reshape(TILE, HD).astype(f32)
+        q = q_buf[head, rows].reshape(TILE, HD).astype(f32)
+        gs_buf[lanes] = (g * column).astype(bf16)
+        qs_buf[lanes] = (q * (column * SCALE)).astype(bf16)
 
     def backward_tile(tile):
         blocks = range(max(0, tile - 4), 1 + min(3, tile)) if tile < 8 else range(3, 4)
@@ -244,7 +273,7 @@
             dst_ref=ret_recv.at[side, slot],
             send_sem=ret_ssem.at[side, slot],
             recv_sem=ret_rsem.at[side, slot],
-            device_id=(jnp.where(slot == 4, after, before), h),
+            device_id=(after if slot == 4 else before, h),
             device_id_type=MESH,
         )
 
@@ -270,12 +299,21 @@
             ).start()
 
     def send_sum(tile):
+        @pl.when(has_after)
+        def _():
+            for side in range(2):
+                give_back(side, tile).wait_recv()
+
+        if tile == 0:
+            @pl.when(has_before)
+            def _():
+                for side in range(2):
+                    give_back(side, 4).wait_recv()
+
         for side in range(2):
-            give_back(side, tile).wait_recv()
             acc = (dk_acc, dv_acc)[side]
             total = acc[4 + tile] + ret_recv[side, tile].astype(f32)
             if tile == 0:
-                give_back(side, 4).wait_recv()
                 total += ret_recv[side, 4].astype(f32)
             own_buf[side, 2 * tile : 2 * tile + 2] = total.astype(bf16).reshape(2, PIECE, HD)
             for part in range(2):
@@ -285,7 +323,7 @@
         tile = 8 if slot == 4 else slot
         for side in range(2):
             ret_send[side, slot] = (dk_acc, dv_acc)[side][tile].astype(bf16)
-            give_back(side, slot).start()
+            pl.when(has_after if slot == 4 else has_before)(give_back(side, slot).start)
 
     @pl.loop(0, 2)
     def _(head):
@@ -295,38 +333,52 @@
                 dst = (q_buf, g_buf)[kind].at[head, source]
                 pltpu.make_async_copy(dst, dst, in_rsem.at[2 + 2 * head + kind, source]).wait()
 
-        for i in (3, 2, 1, 0):
+        for pair in ((3, 2), (1, 0)):
             @pl.when(head == 0)
             def _():
-                for piece in (2 * i, 2 * i + 1):
-                    for side in range(2):
-                        forward(side, piece).wait_recv()
-                turn(i)
-                if i == 3:
-                    for piece in range(2):
-                        for side in range(2):
-                            ahead(side, piece).wait_recv()
-                    for tile in range(4, 9):
-                        turn(tile)
-
-            forward_block(head, i)
-            for part in range(2):
-                send_out(0, head, 2 * i + part)
-
-        for tile in (0, 1, 2, 3, 8, 4, 5, 6, 7):
-            backward_tile(tile)
-            if tile in (0, 1, 2, 3, 8):
+                @pl.when(has_before)
+                def _():
+                    for tile in pair:
+                        for piece in (2 * tile, 2 * tile + 1):
+                            for side in range(2):
+                                forward(side, piece).wait_recv()
+
+                for tile in pair:
+                    turn(tile)
+                if pair[0] == 3:
+                    @pl.when(has_after)
+                    def _():
+                        for piece in range(2):
+                            for side in range(2):
+                                ahead(side, piece).wait_recv()
+
+                    turn(8)
+
+            tops = [scores(head, i) for i in pair]
+            for i, top in zip(pair, tops):
+                attend(head, i, top)
+            for i in pair:
+                for part in range(2):
+                    send_out(0, head, 2 * i + part)
+
+        for group in ((0, 1), (2, 3, 8), (4, 5), (6, 7)):
+            for tile in group:
+                backward_tile(tile)
+            if group[0] < 4:
                 @pl.when(head == 1)
                 def _():
-                    send_back(min(tile, 4))
+                    for tile in group:
+                        send_back(min(tile, 4))
             else:
-                grad_queries(head, tile - 4)
-                for part in range(2):
-                    send_out(1, head, 2 * (tile - 4) + part)
-            if tile in (6, 7):
+                for tile in group:
+                    grad_queries(head, tile - 4)
+                for tile in group:
+                    for part in range(2):
+                        send_out(1, head, 2 * (tile - 4) + part)
+            if group[0] == 6:
                 @pl.when(head == 1)
                 def _():
-                    for own in ((0, 1) if tile == 6 else (2, 3)):
+                    for own in range(4):
                         send_sum(own)
 
     @pl.loop(0, n)
@@ -337,7 +389,7 @@
                 pltpu.make_async_copy(dst, dst, out_rsem.at[kind, head, other]).wait()
             dst = own_dst(kind, other)
             pltpu.make_async_copy(dst, dst, own_rsem.at[kind, other]).wait()
-            forward(kind, other).wait_send()
+            pl.when(has_after)(forward(kind, other).wait_send)
 
         @pl.when(other != h)
         def _():
@@ -351,15 +403,11 @@
                 src = own_buf.at[kind, other]
                 pltpu.make_async_copy(src, src, own_ssem.at[kind, other]).wait()
 
-    @pl.loop(0, 5)
-    def _(slot):
-        for side in range(2):
-            give_back(side, slot).wait_send()
-
-    @pl.loop(0, 2)
-    def _(piece):
-        for side in range(2):
-            ahead(side, piece).wait_send()
+    for side in range(2):
+        for slot in range(5):
+            pl.when(has_after if slot == 4 else has_before)(give_back(side, slot).wait_send)
+        for piece in range(2):
+            pl.when(has_before)(ahead(side, piece).wait_send)
 
 
 def place_results(*refs):
@@ -397,7 +445,7 @@
             pltpu.VMEM((18, PIECE, HD), bf16),
             pltpu.VMEM((HD, WINDOW), bf16),
             pltpu.VMEM((HD, WINDOW), bf16),
-            pltpu.VMEM((6, TILE, TILE), f32),
+            pltpu.VMEM((2, 6, TILE, TILE), f32),
             pltpu.VMEM((WINDOW, BLK), bf16),
             pltpu.VMEM((WINDOW, BLK), bf16),
             pltpu.VMEM((HD, BLK), bf16),

time: 65.9 us -> 59.8 us (0.907)
  Pallas kernels: 65.1 us -> 59 us
    pallas_call x1, Pallas kernels: 62.9 us -> 56.8 us  [local(): pl.pallas_call(kernel, out_shape=[jax.ShapeDtypeStruct(queries.shape, bf1...]
where the time goes in v4:
time: 59.8 us; the launch traced here: 59.6 us
  Pallas kernels  59 us (99%)
  between operations  0.64 us (1%)
    pallas_call x1, Pallas kernels, local(): pl.pallas_call(kernel, out_shape=[jax.ShapeDtypeStruct(queries.shape, bf1...  56.8 us
    pallas_call x1, Pallas kernels, local(): pl.pallas_call(place_results, out_shape=[jax.ShapeDtypeStruct(r.shape, r....  2.25 us

profile of v4, /device:TPU:7, one launch (start us, length us, event | category | flops | bytes accessed | tf_op | source)
XLA Modules:
  0.0 59.6 jit_solution(5281658592560405263)
XLA Ops:
  0.6 56.8 %shard_map.93 = (bf16[128,2048]{1,0:T(8,128)(2,1)}, bf16[128,2048]{1,0:T(8,128)(2,1)}, bf16[128,1024]{1,0:T(8,128)(2,1)}, bf16[128,1024]{1,0:T(8,128)(2,1)}) custom-call(bf16[128,2048]{1,0:T(8,128)(2,1)} %q_hbm.1, bf16[128,1024]{1,0:T(8,128)(2,1)} %k_hbm.1, bf16[128,1024]{1,0:T(8,128)(2,1)} %v_hbm.1, bf16[128,2048]{1,0:T(8,128)(2,1)} %g_hbm.1, ...), custom_call_target="tpu_custom_call" | custom-call | tf_op jit(solution)/shard_map/pallas_call | solution.py:429
  57.4 2.2 %shard_map.94 = (bf16[128,2048]{1,0:T(8,128)(2,1)}, bf16[128,2048]{1,0:T(8,128)(2,1)}, bf16[128,1024]{1,0:T(8,128)(2,1)}, bf16[128,1024]{1,0:T(8,128)(2,1)}) custom-call(bf16[128,2048]{1,0:T(8,128)(2,1)} %get-tuple-element.8.refs_0_, bf16[128,2048]{1,0:T(8,128)(2,1)} %get-tuple-element.9.refs_1_, bf16[128,1024]{1,0:T(8,128)(2,1)} %get-tuple-element.10.refs_2_, ...), custom_call_target="tpu_custom_call" | custom-call | tf_op jit(solution)/shard_map/pallas_call | solution.py:489

commit v5 on v4

--- a/solution.py
+++ b/solution.py
@@ -78,24 +78,32 @@
             return (k_win, v_win)[stream].at[8 + source]
         return (q_buf, g_buf)[stream % 2].at[(stream - 2) // 2, source]
 
-    def send_in(streams):
+    core = lax.rem(h, 2)
+    turns = (((1, 0), (3, 0)), ((1, 1), (3, 1)), ((2, 0), (2, 1)), ((0, 1),))
+
+    def partner(step, other):
+        chip = lax.rem(h // 2 + 4 + (1 - 2 * core) * step, 4)
+        return 2 * chip + (1 - core if other else core)
+
+    def send_in(streams, which):
+        for turn_of in which:
+            for stream in streams:
+                for step, other in turn_of:
+                    target = partner(step, other)
+                    pltpu.make_async_remote_copy(
+                        src_ref=in_src(stream, target),
+                        dst_ref=in_dst(stream, h),
+                        send_sem=in_ssem.at[stream, target],
+                        recv_sem=in_rsem.at[stream, h],
+                        device_id=(c, target),
+                        device_id_type=MESH,
+                    ).start()
+
+    def keep_in(streams):
         for stream in streams:
             pltpu.make_async_copy(
                 in_src(stream, h), in_dst(stream, h), in_rsem.at[stream, h]
             ).start()
-
-        @pl.loop(1, n)
-        def _(r):
-            target = lax.rem(h + r, n)
-            for stream in streams:
-                pltpu.make_async_remote_copy(
-                    src_ref=in_src(stream, target),
-                    dst_ref=in_dst(stream, h),
-                    send_sem=in_ssem.at[stream, target],
-                    recv_sem=in_rsem.at[stream, h],
-                    device_id=(c, target),
-                    device_id_type=MESH,
-                ).start()
 
     def wait_in(stream, source):
         dst = in_dst(stream, source)
@@ -131,11 +139,15 @@
         mark.start()
     stages[0].wait()
     stages[1].wait()
-    send_in((0, 1))
+    send_in((0, 1), turns)
+    keep_in((0, 1))
     stages[2].wait()
     stages[3].wait()
-    send_in((2, 3))
-    for piece in (7, 6, 0, 1, 5, 4, 3, 2):
+    send_in((2, 3), turns[:1])
+    keep_in((2, 3, 4, 5))
+    for place_in, piece in enumerate((7, 6, 0, 1, 5, 4, 3, 2)):
+        if place_in in (2, 4, 6):
+            send_in((2, 3), turns[place_in // 2 : place_in // 2 + 1])
         for side in range(2):
             wait_in(side, piece)
             if piece >= 2:
@@ -149,7 +161,7 @@
             for side in range(2):
                 forward(side, piece).start()
 
-    send_in((4, 5))
+    send_in((4, 5), turns)
 
     @pl.when(jnp.logical_not(has_before))
     def _():
@@ -249,23 +261,21 @@
         cols = pl.ds(pl.multiple_of(source * 2 * HD + head * HD, HD), HD)
         return (o_hbm, gq_hbm)[kind].at[:, cols]
 
-    def send_out(kind, head, target):
-        @pl.when(target == h)
-        def _():
-            pltpu.make_async_copy(
-                out_src(kind, head, target), out_dst(kind, head, h), out_rsem.at[kind, head, h]
-            ).start()
-
-        @pl.when(target != h)
-        def _():
-            pltpu.make_async_remote_copy(
-                src_ref=out_src(kind, head, target),
-                dst_ref=out_dst(kind, head, h),
-                send_sem=out_ssem.at[kind, head, target],
-                recv_sem=out_rsem.at[kind, head, h],
-                device_id=(c, target),
-                device_id_type=MESH,
-            ).start()
+    def send_out(kind, head):
+        pltpu.make_async_copy(
+            out_src(kind, head, h), out_dst(kind, head, h), out_rsem.at[kind, head, h]
+        ).start()
+        for turn_of in turns:
+            for step, other in turn_of:
+                target = partner(step, other)
+                pltpu.make_async_remote_copy(
+                    src_ref=out_src(kind, head, target),
+                    dst_ref=out_dst(kind, head, h),
+                    send_sem=out_ssem.at[kind, head, target],
+                    recv_sem=out_rsem.at[kind, head, h],
+                    device_id=(c, target),
+                    device_id_type=MESH,
+                ).start()
 
     def give_back(side, slot):
         return pltpu.make_async_remote_copy(
@@ -280,25 +290,23 @@
     def own_dst(side, source):
         return (gk_hbm, gv_hbm)[side].at[:, pl.ds(pl.multiple_of(source * HD, HD), HD)]
 
-    def send_own(side, target):
-        @pl.when(target == h)
-        def _():
-            pltpu.make_async_copy(
-                own_buf.at[side, target], own_dst(side, h), own_rsem.at[side, h]
-            ).start()
-
-        @pl.when(target != h)
-        def _():
-            pltpu.make_async_remote_copy(
-                src_ref=own_buf.at[side, target],
-                dst_ref=own_dst(side, h),
-                send_sem=own_ssem.at[side, target],
-                recv_sem=own_rsem.at[side, h],
-                device_id=(c, target),
-                device_id_type=MESH,
-            ).start()
-
-    def send_sum(tile):
+    def send_own():
+        for side in range(2):
+            pltpu.make_async_copy(own_buf.at[side, h], own_dst(side, h), own_rsem.at[side, h]).start()
+        for turn_of in turns:
+            for side in range(2):
+                for step, other in turn_of:
+                    target = partner(step, other)
+                    pltpu.make_async_remote_copy(
+                        src_ref=own_buf.at[side, target],
+                        dst_ref=own_dst(side, h),
+                        send_sem=own_ssem.at[side, target],
+                        recv_sem=own_rsem.at[side, h],
+                        device_id=(c, target),
+                        device_id_type=MESH,
+                    ).start()
+
+    def add_up(tile):
         @pl.when(has_after)
         def _():
             for side in range(2):
@@ -316,8 +324,6 @@
             if tile == 0:
                 total += ret_recv[side, 4].astype(f32)
             own_buf[side, 2 * tile : 2 * tile + 2] = total.astype(bf16).reshape(2, PIECE, HD)
-            for part in range(2):
-                send_own(side, 2 * tile + part)
 
     def send_back(slot):
         tile = 8 if slot == 4 else slot
@@ -357,10 +363,8 @@
             tops = [scores(head, i) for i in pair]
             for i, top in zip(pair, tops):
                 attend(head, i, top)
-            for i in pair:
-                for part in range(2):
-                    send_out(0, head, 2 * i + part)
-
+
+        send_out(0, head)
         for group in ((0, 1), (2, 3, 8), (4, 5), (6, 7)):
             for tile in group:
                 backward_tile(tile)
@@ -372,14 +376,12 @@
             else:
                 for tile in group:
                     grad_queries(head, tile - 4)
-                for tile in group:
-                    for part in range(2):
-                        send_out(1, head, 2 * (tile - 4) + part)
-            if group[0] == 6:
-                @pl.when(head == 1)
-                def _():
-                    for own in range(4):
-                        send_sum(own)
+
+        send_out(1, head)
+
+    for tile in range(4):
+        add_up(tile)
+    send_own()
 
     @pl.loop(0, n)
     def _(other):

time: 59.8 us -> 62 us (1.037); the launches traced: 59.6 us -> 61.1 us
  Pallas kernels: 59 us -> 60.4 us
    pallas_call x1, Pallas kernels: 56.8 us -> 58.2 us  [local(): pl.pallas_call(kernel, out_shape=[jax.ShapeDtypeStruct(queries.shape, bf1...]
where the time goes in v5:
time: 62 us; the launch traced here: 61.1 us
  Pallas kernels  60.4 us (97%)
  between operations  0.64 us (1%)
    pallas_call x1, Pallas kernels, local(): pl.pallas_call(kernel, out_shape=[jax.ShapeDtypeStruct(queries.shape, bf1...  58.2 us
    pallas_call x1, Pallas kernels, local(): pl.pallas_call(place_results, out_shape=[jax.ShapeDtypeStruct(r.shape, r....  2.25 us

profile of v5, /device:TPU:7, one launch (start us, length us, event | category | flops | bytes accessed | tf_op | source)
XLA Modules:
  0.0 61.1 jit_solution(18052189512777946927)
XLA Ops:
  0.6 58.2 %shard_map.93 = (bf16[128,2048]{1,0:T(8,128)(2,1)}, bf16[128,2048]{1,0:T(8,128)(2,1)}, bf16[128,1024]{1,0:T(8,128)(2,1)}, bf16[128,1024]{1,0:T(8,128)(2,1)}) custom-call(bf16[128,2048]{1,0:T(8,128)(2,1)} %q_hbm.1, bf16[128,1024]{1,0:T(8,128)(2,1)} %k_hbm.1, bf16[128,1024]{1,0:T(8,128)(2,1)} %v_hbm.1, bf16[128,2048]{1,0:T(8,128)(2,1)} %g_hbm.1, ...), custom_call_target="tpu_custom_call" | custom-call | tf_op jit(solution)/shard_map/pallas_call | solution.py:431
  58.8 2.2 %shard_map.94 = (bf16[128,2048]{1,0:T(8,128)(2,1)}, bf16[128,2048]{1,0:T(8,128)(2,1)}, bf16[128,1024]{1,0:T(8,128)(2,1)}, bf16[128,1024]{1,0:T(8,128)(2,1)}) custom-call(bf16[128,2048]{1,0:T(8,128)(2,1)} %get-tuple-element.8.refs_0_, bf16[128,2048]{1,0:T(8,128)(2,1)} %get-tuple-element.9.refs_1_, bf16[128,1024]{1,0:T(8,128)(2,1)} %get-tuple-element.10.refs_2_, ...), custom_call_target="tpu_custom_call" | custom-call | tf_op jit(solution)/shard_map/pallas_call | solution.py:491

commit v6 on v4

--- a/solution.py
+++ b/solution.py
@@ -185,7 +185,7 @@
     def scores(head, i):
         rows = pl.ds(2 * i, 2)
         qt = q_buf[head, rows].reshape(TILE, HD).T
-        gt_buf[:, pl.ds(i * TILE, TILE)] = g_buf[head, rows].reshape(TILE, HD).T
+        gt_buf[head, :, pl.ds(i * TILE, TILE)] = g_buf[head, rows].reshape(TILE, HD).T
         first = (c - 1) * BLK + i * TILE
         lower = lower_ref[i] - first
         upper = upper_ref[i] - first
@@ -209,37 +209,40 @@
         total = None
         for t in range(tiles):
             p = jnp.exp2(s_buf[i % 2, t] - top)
-            p_buf[pl.ds((i + t) * TILE, TILE), lanes] = p.astype(bf16)
+            p_buf[head, pl.ds((i + t) * TILE, TILE), lanes] = p.astype(bf16)
             part = jnp.sum(p, axis=0, keepdims=True)
             total = part if total is None else total + part
         share = 1.0 / total
-        out = (matmul(vt_win[:, window], p_buf[window, lanes]) * share).astype(bf16)
+        out = (matmul(vt_win[:, window], p_buf[head, window, lanes]) * share).astype(bf16)
         o_buf[head, rows] = out.T.reshape(2, PIECE, HD)
-        gt = gt_buf[:, lanes].astype(f32)
-        delta_buf[i] = jnp.sum(gt * out.astype(f32), axis=0, keepdims=True)
-        scaled_buf[i] = share * SCALE
+        gt = gt_buf[head, :, lanes].astype(f32)
+        delta_buf[head, i] = jnp.sum(gt * out.astype(f32), axis=0, keepdims=True)
+        scaled_buf[head, i] = share * SCALE
         column = jnp.broadcast_to(share, (8, TILE)).T[:, :1]
         g = g_buf[head, rows].reshape(TILE, HD).astype(f32)
         q = q_buf[head, rows].reshape(TILE, HD).astype(f32)
-        gs_buf[lanes] = (g * column).astype(bf16)
-        qs_buf[lanes] = (q * (column * SCALE)).astype(bf16)
-
-    def backward_tile(tile):
-        blocks = range(max(0, tile - 4), 1 + min(3, tile)) if tile < 8 else range(3, 4)
+        gs_buf[head, lanes] = (g * column).astype(bf16)
+        qs_buf[head, lanes] = (q * (column * SCALE)).astype(bf16)
+
+    def backward_tile(head, tile, blocks=range(4)):
+        reach = range(max(0, tile - 4), 1 + min(3, tile)) if tile < 8 else range(3, 4)
+        blocks = [i for i in reach if i in blocks]
         rows = pl.ds(tile * TILE, TILE)
         span = pl.ds(blocks[0] * TILE, len(blocks) * TILE)
         v = values(tile)
-        dv_acc[tile] += matmul(p_buf[rows, span], gs_buf[span])
+        dv_acc[tile] += matmul(p_buf[head, rows, span], gs_buf[head, span])
         for i in blocks:
             lanes = pl.ds(i * TILE, TILE)
-            dp = matmul(v, gt_buf[:, lanes])
-            ds_buf[rows, lanes] = p_buf[rows, lanes] * (dp - delta_buf[i]).astype(bf16)
-        dk_acc[tile] += matmul(ds_buf[rows, span], qs_buf[span])
+            dp = matmul(v, gt_buf[head, :, lanes])
+            ds_buf[head, rows, lanes] = p_buf[head, rows, lanes] * (
+                dp - delta_buf[head, i]
+            ).astype(bf16)
+        dk_acc[tile] += matmul(ds_buf[head, rows, span], qs_buf[head, span])
 
     def grad_queries(head, i):
         lanes = pl.ds(i * TILE, TILE)
         window = pl.ds(i * TILE, (6 if i == 3 else 5) * TILE)
-        grad = matmul(kt_win[:, window], ds_buf[window, lanes]) * scaled_buf[i]
+        grad = matmul(kt_win[:, window], ds_buf[head, window, lanes]) * scaled_buf[head, i]
         gq_buf[head, pl.ds(2 * i, 2)] = grad.astype(bf16).T.reshape(2, PIECE, HD)
 
     def out_src(kind, head, target):
@@ -325,61 +328,78 @@
             ret_send[side, slot] = (dk_acc, dv_acc)[side][tile].astype(bf16)
             pl.when(has_after if slot == 4 else has_before)(give_back(side, slot).start)
 
-    @pl.loop(0, 2)
-    def _(head):
+    def wait_head(head):
         @pl.loop(0, n)
         def _(source):
             for kind in range(2):
-                dst = (q_buf, g_buf)[kind].at[head, source]
-                pltpu.make_async_copy(dst, dst, in_rsem.at[2 + 2 * head + kind, source]).wait()
-
-        for pair in ((3, 2), (1, 0)):
-            @pl.when(head == 0)
-            def _():
-                @pl.when(has_before)
-                def _():
-                    for tile in pair:
-                        for piece in (2 * tile, 2 * tile + 1):
-                            for side in range(2):
-                                forward(side, piece).wait_recv()
-
-                for tile in pair:
-                    turn(tile)
-                if pair[0] == 3:
-                    @pl.when(has_after)
-                    def _():
-                        for piece in range(2):
-                            for side in range(2):
-                                ahead(side, piece).wait_recv()
-
-                    turn(8)
-
-            tops = [scores(head, i) for i in pair]
-            for i, top in zip(pair, tops):
-                attend(head, i, top)
-            for i in pair:
-                for part in range(2):
-                    send_out(0, head, 2 * i + part)
-
-        for group in ((0, 1), (2, 3, 8), (4, 5), (6, 7)):
-            for tile in group:
-                backward_tile(tile)
-            if group[0] < 4:
-                @pl.when(head == 1)
-                def _():
-                    for tile in group:
-                        send_back(min(tile, 4))
-            else:
-                for tile in group:
-                    grad_queries(head, tile - 4)
-                for tile in group:
-                    for part in range(2):
-                        send_out(1, head, 2 * (tile - 4) + part)
-            if group[0] == 6:
-                @pl.when(head == 1)
-                def _():
-                    for own in range(4):
-                        send_sum(own)
+                wait_in(2 + 2 * head + kind, source)
+
+    def wait_prior(tiles):
+        @pl.when(has_before)
+        def _():
+            for tile in tiles:
+                for piece in (2 * tile, 2 * tile + 1):
+                    for side in range(2):
+                        forward(side, piece).wait_recv()
+
+        for tile in tiles:
+            turn(tile)
+
+    def forward_pair(head, pair):
+        tops = [scores(head, i) for i in pair]
+        for i, top in zip(pair, tops):
+            attend(head, i, top)
+        for i in pair:
+            for part in range(2):
+                send_out(0, head, 2 * i + part)
+
+    def send_grad(head, blocks):
+        for i in blocks:
+            for part in range(2):
+                send_out(1, head, 2 * i + part)
+
+    wait_head(0)
+    wait_prior((3, 2))
+
+    @pl.when(has_after)
+    def _():
+        for piece in range(2):
+            for side in range(2):
+                ahead(side, piece).wait_recv()
+
+    turn(8)
+    forward_pair(0, (3, 2))
+    for tile in (8, 4, 5, 6, 7):
+        backward_tile(0, tile, (2, 3))
+    wait_prior((1, 0))
+    forward_pair(0, (1, 0))
+    wait_head(1)
+    forward_pair(1, (3, 2))
+    forward_pair(1, (1, 0))
+    for group in ((0, 1), (2,), (3, 8)):
+        for tile in group:
+            if tile < 8:
+                backward_tile(0, tile)
+            backward_tile(1, tile)
+        for tile in group:
+            send_back(min(tile, 4))
+    backward_tile(0, 4, (0, 1))
+    backward_tile(0, 5, (1,))
+    for i in range(4):
+        grad_queries(0, i)
+    send_grad(0, range(4))
+    backward_tile(1, 4)
+    backward_tile(1, 5)
+    grad_queries(1, 0)
+    grad_queries(1, 1)
+    send_grad(1, (0, 1))
+    backward_tile(1, 6)
+    backward_tile(1, 7)
+    grad_queries(1, 2)
+    grad_queries(1, 3)
+    send_grad(1, (2, 3))
+    for tile in range(4):
+        send_sum(tile)
 
     @pl.loop(0, n)
     def _(other):
@@ -446,13 +466,13 @@
             pltpu.VMEM((HD, WINDOW), bf16),
             pltpu.VMEM((HD, WINDOW), bf16),
             pltpu.VMEM((2, 6, TILE, TILE), f32),
-            pltpu.VMEM((WINDOW, BLK), bf16),
-            pltpu.VMEM((WINDOW, BLK), bf16),
-            pltpu.VMEM((HD, BLK), bf16),
-            pltpu.VMEM((BLK, HD), bf16),
-            pltpu.VMEM((BLK, HD), bf16),
-            pltpu.VMEM((4, 1, TILE), f32),
-            pltpu.VMEM((4, 1, TILE), f32),
+            pltpu.VMEM((2, WINDOW, BLK), bf16),
+            pltpu.VMEM((2, WINDOW, BLK), bf16),
+            pltpu.VMEM((2, HD, BLK), bf16),
+            pltpu.VMEM((2, BLK, HD), bf16),
+            pltpu.VMEM((2, BLK, HD), bf16),
+            pltpu.VMEM((2, 4, 1, TILE), f32),
+            pltpu.VMEM((2, 4, 1, TILE), f32),
             pltpu.VMEM((9, TILE, HD), f32),
             pltpu.VMEM((9, TILE, HD), f32),
             pltpu.VMEM((2, 8, PIECE, HD), bf16),

time: 59.8 us -> 56.9 us (0.952)
  Pallas kernels: 59 us -> 55.9 us
    pallas_call x1, Pallas kernels: 56.8 us -> 53.6 us  [local(): pl.pallas_call(kernel, out_shape=[jax.ShapeDtypeStruct(queries.shape, bf1...]
where the time goes in v6:
time: 56.9 us; the launch traced here: 56.7 us
  Pallas kernels  55.9 us (98%)
  between operations  0.8 us (1%)
    pallas_call x1, Pallas kernels, local(): pl.pallas_call(kernel, out_shape=[jax.ShapeDtypeStruct(queries.shape, bf1...  53.6 us
    pallas_call x1, Pallas kernels, local(): pl.pallas_call(place_results, out_shape=[jax.ShapeDtypeStruct(r.shape, r....  2.25 us

profile of v6, /device:TPU:7, one launch (start us, length us, event | category | flops | bytes accessed | tf_op | source)
XLA Modules:
  0.0 56.7 jit_solution(13465146383653018702)
XLA Ops:
  0.6 53.6 %shard_map.93 = (bf16[128,2048]{1,0:T(8,128)(2,1)}, bf16[128,2048]{1,0:T(8,128)(2,1)}, bf16[128,1024]{1,0:T(8,128)(2,1)}, bf16[128,1024]{1,0:T(8,128)(2,1)}) custom-call(bf16[128,2048]{1,0:T(8,128)(2,1)} %q_hbm.1, bf16[128,1024]{1,0:T(8,128)(2,1)} %k_hbm.1, bf16[128,1024]{1,0:T(8,128)(2,1)} %v_hbm.1, bf16[128,2048]{1,0:T(8,128)(2,1)} %g_hbm.1, ...), custom_call_target="tpu_custom_call" | custom-call | tf_op jit(solution)/shard_map/pallas_call | solution.py:449
  54.3 2.2 %shard_map.94 = (bf16[128,2048]{1,0:T(8,128)(2,1)}, bf16[128,2048]{1,0:T(8,128)(2,1)}, bf16[128,1024]{1,0:T(8,128)(2,1)}, bf16[128,1024]{1,0:T(8,128)(2,1)}) custom-call(bf16[128,2048]{1,0:T(8,128)(2,1)} %get-tuple-element.8.refs_0_, bf16[128,2048]{1,0:T(8,128)(2,1)} %get-tuple-element.9.refs_1_, bf16[128,1024]{1,0:T(8,128)(2,1)} %get-tuple-element.10.refs_2_, ...), custom_call_target="tpu_custom_call" | custom-call | tf_op jit(solution)/shard_map/pallas_call | solution.py:509

commit v7 on v6

--- a/solution.py
+++ b/solution.py
@@ -131,6 +131,19 @@
         mark.start()
     stages[0].wait()
     stages[1].wait()
+
+    @pl.when(has_after)
+    def _():
+        for side in range(2):
+            pltpu.make_async_remote_copy(
+                src_ref=in_src(side, h),
+                dst_ref=(k_win, v_win)[side].at[h],
+                send_sem=fwd_ssem.at[side, h],
+                recv_sem=fwd_rsem.at[side, h],
+                device_id=(after, h),
+                device_id_type=MESH,
+            ).start()
+
     send_in((0, 1))
     stages[2].wait()
     stages[3].wait()
@@ -139,15 +152,13 @@
         for side in range(2):
             wait_in(side, piece)
             if piece >= 2:
-                pl.when(has_after)(forward(side, piece).start)
+                pl.when(has_after & (h != piece))(forward(side, piece).start)
             else:
                 pl.when(has_before)(ahead(side, piece).start)
 
-    @pl.when(has_after)
-    def _():
-        for piece in (1, 0):
-            for side in range(2):
-                forward(side, piece).start()
+    for piece in (1, 0):
+        for side in range(2):
+            pl.when(has_after & (h != piece))(forward(side, piece).start)
 
     send_in((4, 5))
 
@@ -373,16 +384,20 @@
         backward_tile(0, tile, (2, 3))
     wait_prior((1, 0))
     forward_pair(0, (1, 0))
+    backward_tile(0, 0)
+    backward_tile(0, 1)
     wait_head(1)
+    forward_pair(1, (1, 0))
+    for tile in (0, 1):
+        backward_tile(1, tile)
+        send_back(tile)
     forward_pair(1, (3, 2))
-    forward_pair(1, (1, 0))
-    for group in ((0, 1), (2,), (3, 8)):
-        for tile in group:
-            if tile < 8:
-                backward_tile(0, tile)
-            backward_tile(1, tile)
-        for tile in group:
-            send_back(min(tile, 4))
+    for tile in (2, 3):
+        backward_tile(0, tile)
+        backward_tile(1, tile)
+        send_back(tile)
+    backward_tile(1, 8)
+    send_back(4)
     backward_tile(0, 4, (0, 1))
     backward_tile(0, 5, (1,))
     for i in range(4):

time: 56.9 us -> 53.7 us (0.944)
  Pallas kernels: 55.9 us -> 52.2 us
    pallas_call x1, Pallas kernels: 53.6 us -> 50 us  [local(): pl.pallas_call(kernel, out_shape=[jax.ShapeDtypeStruct(queries.shape, bf1...]
where the time goes in v7:
time: 53.7 us; the launch traced here: 53 us
  Pallas kernels  52.2 us (97%)
  between operations  0.8 us (1%)
    pallas_call x1, Pallas kernels, local(): pl.pallas_call(kernel, out_shape=[jax.ShapeDtypeStruct(queries.shape, bf1...  50 us
    pallas_call x1, Pallas kernels, local(): pl.pallas_call(place_results, out_shape=[jax.ShapeDtypeStruct(r.shape, r....  2.25 us

profile of v7, /device:TPU:7, one launch (start us, length us, event | category | flops | bytes accessed | tf_op | source)
XLA Modules:
  0.0 53.0 jit_solution(2790380249419209741)
XLA Ops:
  0.6 50.0 %shard_map.93 = (bf16[128,2048]{1,0:T(8,128)(2,1)}, bf16[128,2048]{1,0:T(8,128)(2,1)}, bf16[128,1024]{1,0:T(8,128)(2,1)}, bf16[128,1024]{1,0:T(8,128)(2,1)}) custom-call(bf16[128,2048]{1,0:T(8,128)(2,1)} %q_hbm.1, bf16[128,1024]{1,0:T(8,128)(2,1)} %k_hbm.1, bf16[128,1024]{1,0:T(8,128)(2,1)} %v_hbm.1, bf16[128,2048]{1,0:T(8,128)(2,1)} %g_hbm.1, ...), custom_call_target="tpu_custom_call" | custom-call | tf_op jit(solution)/shard_map/pallas_call | solution.py:464
  50.6 2.2 %shard_map.94 = (bf16[128,2048]{1,0:T(8,128)(2,1)}, bf16[128,2048]{1,0:T(8,128)(2,1)}, bf16[128,1024]{1,0:T(8,128)(2,1)}, bf16[128,1024]{1,0:T(8,128)(2,1)}) custom-call(bf16[128,2048]{1,0:T(8,128)(2,1)} %get-tuple-element.8.refs_0_, bf16[128,2048]{1,0:T(8,128)(2,1)} %get-tuple-element.9.refs_1_, bf16[128,1024]{1,0:T(8,128)(2,1)} %get-tuple-element.10.refs_2_, ...), custom_call_target="tpu_custom_call" | custom-call | tf_op jit(solution)/shard_map/pallas_call | solution.py:524

commit v8 on v7

--- a/solution.py
+++ b/solution.py
@@ -387,8 +387,8 @@
     backward_tile(0, 0)
     backward_tile(0, 1)
     wait_head(1)
-    forward_pair(1, (1, 0))
     for tile in (0, 1):
+        forward_pair(1, (tile,))
         backward_tile(1, tile)
         send_back(tile)
     forward_pair(1, (3, 2))
@@ -408,12 +408,13 @@
     grad_queries(1, 0)
     grad_queries(1, 1)
     send_grad(1, (0, 1))
+    send_sum(1)
     backward_tile(1, 6)
     backward_tile(1, 7)
     grad_queries(1, 2)
     grad_queries(1, 3)
     send_grad(1, (2, 3))
-    for tile in range(4):
+    for tile in (0, 2, 3):
         send_sum(tile)
 
     @pl.loop(0, n)

time: 53.7 us -> 54.3 us (1.011)
  Pallas kernels: 52.2 us -> 52.8 us
    pallas_call x1, Pallas kernels: 50 us -> 50.6 us  [local(): pl.pallas_call(kernel, out_shape=[jax.ShapeDtypeStruct(queries.shape, bf1...]
where the time goes in v8:
time: 54.3 us; the launch traced here: 53.6 us
  Pallas kernels  52.8 us (97%)
  between operations  0.8 us (1%)
    pallas_call x1, Pallas kernels, local(): pl.pallas_call(kernel, out_shape=[jax.ShapeDtypeStruct(queries.shape, bf1...  50.6 us
    pallas_call x1, Pallas kernels, local(): pl.pallas_call(place_results, out_shape=[jax.ShapeDtypeStruct(r.shape, r....  2.25 us

profile of v8, /device:TPU:7, one launch (start us, length us, event | category | flops | bytes accessed | tf_op | source)
XLA Modules:
  0.0 53.6 jit_solution(7085601503128248327)
XLA Ops:
  0.6 50.6 %shard_map.93 = (bf16[128,2048]{1,0:T(8,128)(2,1)}, bf16[128,2048]{1,0:T(8,128)(2,1)}, bf16[128,1024]{1,0:T(8,128)(2,1)}, bf16[128,1024]{1,0:T(8,128)(2,1)}) custom-call(bf16[128,2048]{1,0:T(8,128)(2,1)} %q_hbm.1, bf16[128,1024]{1,0:T(8,128)(2,1)} %k_hbm.1, bf16[128,1024]{1,0:T(8,128)(2,1)} %v_hbm.1, bf16[128,2048]{1,0:T(8,128)(2,1)} %g_hbm.1, ...), custom_call_target="tpu_custom_call" | custom-call | tf_op jit(solution)/shard_map/pallas_call | solution.py:465
  51.2 2.2 %shard_map.94 = (bf16[128,2048]{1,0:T(8,128)(2,1)}, bf16[128,2048]{1,0:T(8,128)(2,1)}, bf16[128,1024]{1,0:T(8,128)(2,1)}, bf16[128,1024]{1,0:T(8,128)(2,1)}) custom-call(bf16[128,2048]{1,0:T(8,128)(2,1)} %get-tuple-element.8.refs_0_, bf16[128,2048]{1,0:T(8,128)(2,1)} %get-tuple-element.9.refs_1_, bf16[128,1024]{1,0:T(8,128)(2,1)} %get-tuple-element.10.refs_2_, ...), custom_call_target="tpu_custom_call" | custom-call | tf_op jit(solution)/shard_map/pallas_call | solution.py:525
